TPU v7x, 32 devices: a whole 2x2x4 slice. The times are simulated.
32 devices in a mesh: dp: 8 (over y, x, core), seq: 4 (over z).
Axes of the slice: x: 2, y: 2, z: 4, core: 2. Of those that a mesh axis runs over, the one named last changes fastest.
Arguments:
- tokens: bfloat16 [32768, 512], P(('dp', 'seq')), may hold values from -6 to 6
- routes: int32 [32768, 2], P(('dp', 'seq')), may hold values from 0 to 7, all different within a row
- lengths: int32 [8, 13], P('dp'), may hold values from 1 to 4084, as said below
- cotangent: bfloat16 [32768, 512], P(('dp', 'seq')), may hold values from -6 to 6
- first_gain: float32 [512], P(('dp', 'seq')), may hold values from 0.5 to 1.5
- first_shift: float32 [512], P(('dp', 'seq')), may hold values from -1.25 to 1.25
- router: float32 [512, 8], P(('dp', 'seq')), may hold values from -0.21875 to 0.21875
- query_map: float32 [512, 512], P(('dp', 'seq')), may hold values from -0.375 to 0.375
- keyval: float32 [512, 128], P(('dp', 'seq')), may hold values from -0.375 to 0.375
- output_map: float32 [512, 512], P(('dp', 'seq')), may hold values from -2 to 2
- second_gain: float32 [512], P(('dp', 'seq')), may hold values from 0.5 to 1.5
- second_shift: float32 [512], P(('dp', 'seq')), may hold values from -1.25 to 1.25
- expand: float32 [512, 2048], P(('dp', 'seq')), may hold values from -0.25 to 0.25
- expand_bias: float32 [2048], P(('dp', 'seq')), may hold values from -1.75 to 1.75
- contract: float32 [2048, 512], P(('dp', 'seq')), may hold values from -0.125 to 0.125
- contract_bias: float32 [512], P(('dp', 'seq')), may hold values from -1.75 to 1.75
Outputs:
- layer_out: bfloat16 [32768, 512], P(('dp', 'seq'))
- grad_tokens: bfloat16 [32768, 512], P(('dp', 'seq'))
- grad_first_gain: float32 [512], P(('dp', 'seq'))
- grad_first_shift: float32 [512], P(('dp', 'seq'))
- grad_router: float32 [512, 8], P(('dp', 'seq'))
- grad_query_map: float32 [512, 512], P(('dp', 'seq'))
- grad_keyval: float32 [512, 128], P(('dp', 'seq'))
- grad_output_map: float32 [512, 512], P(('dp', 'seq'))
- grad_second_gain: float32 [512], P(('dp', 'seq'))
- grad_second_shift: float32 [512], P(('dp', 'seq'))
- grad_expand: float32 [512, 2048], P(('dp', 'seq'))
- grad_expand_bias: float32 [2048], P(('dp', 'seq'))
- grad_contract: float32 [2048, 512], P(('dp', 'seq'))
- grad_contract_bias: float32 [512], P(('dp', 'seq'))
Inputs may be any that keep to these rules, and one draw needn't show every extreme that they name: `routes`: the 2 experts of a token differ. `lengths`: each row sums to 4096; one entry of each row is larger than 3072, every other entry is at most 64.
All inputs are finite; a program needn't handle non-finite values.
Results may differ from a plain program's by a relative error of at most 0.024.
Values may be sent and summed in bfloat16 or wider, within the bound.
No kernel may reach another device: no remote copies, remote signals or barrier semaphores. Data moves between devices by JAX's collectives and lax.ppermute only.
A program may use at most 128 MiB of HBM per device.

v0:
```python
import jax
import jax.numpy as jnp
from jax import lax
from jax.sharding import PartitionSpec as P


def to_low(matrix):
    return matrix.astype(jnp.bfloat16)


def dot_plain(left_side, right_side):
    return jnp.dot(left_side, right_side, preferred_element_type=jnp.float32)


def dot_last(left_side, right_side):
    return lax.dot_general(
        left_side, right_side, (((1,), (1,)), ((), ())), preferred_element_type=jnp.float32
    )


def dot_first(left_side, right_side):
    return lax.dot_general(
        left_side, right_side, (((0,), (0,)), ((), ())), preferred_element_type=jnp.float32
    )


def norm_rows(matrix, scale_row, shift_row):
    center = matrix - jnp.mean(matrix, axis=-1, keepdims=True)
    spread = jnp.mean(center * center, axis=-1, keepdims=True)
    return center * lax.rsqrt(spread + 1e-05) * scale_row + shift_row


def smooth_gate(matrix):
    return jax.nn.gelu(matrix, approximate=True)


def pick_rows(per_expert, onehot):
    return jnp.sum(per_expert[:, None, :, :] * onehot[:, :, :, None], axis=2)


def spread_rows(per_choice, onehot):
    return jnp.sum(per_choice[:, :, None, :] * onehot[:, :, :, None], axis=1)


def block_scores(query_block, doc_block, key_value, doc_keys, score_scale):
    head_size = query_block.shape[1]
    scores = dot_last(query_block, key_value[:, :head_size]) * score_scale
    same_doc = doc_block[:, None] == doc_keys[None, :]
    return (scores, same_doc)


def attention_forward(query_block, doc_block, keyval_all, doc_all, key_rows, score_scale):
    head_size = query_block.shape[1]

    def advance(block_index, partial_value):
        running_max, running_sum, running_acc = partial_value
        key_value = lax.dynamic_slice_in_dim(keyval_all, block_index * key_rows, key_rows, 0)
        doc_keys = lax.dynamic_slice_in_dim(doc_all, block_index * key_rows, key_rows, 0)
        scores, same_doc = block_scores(query_block, doc_block, key_value, doc_keys, score_scale)
        masked = jnp.where(same_doc, scores, -1e30)
        new_max = jnp.maximum(running_max, jnp.max(masked, axis=1))
        factor = jnp.exp(running_max - new_max)
        weights = jnp.where(same_doc, jnp.exp(masked - new_max[:, None]), 0.0)
        running_sum = running_sum * factor + jnp.sum(weights, axis=1)
        running_acc = running_acc * factor[:, None] + dot_plain(
            to_low(weights), key_value[:, head_size:]
        )
        return (new_max, running_sum, running_acc)

    row_count = query_block.shape[0]
    initial = (
        jnp.full((row_count,), -1e30, jnp.float32),
        jnp.zeros((row_count,), jnp.float32),
        jnp.zeros(query_block.shape, jnp.float32),
    )
    running_max, running_sum, running_acc = lax.fori_loop(
        0, keyval_all.shape[0] // key_rows, advance, initial
    )
    return (running_acc / running_sum[:, None], running_max + jnp.log(running_sum))


def block_backward(
    query_block, doc_block, log_total, delta_rows, grad_attn, key_value, doc_keys, score_scale
):
    head_size = query_block.shape[1]
    scores, same_doc = block_scores(query_block, doc_block, key_value, doc_keys, score_scale)
    probs = jnp.where(
        same_doc, jnp.exp(jnp.where(same_doc, scores, -1e30) - log_total[:, None]), 0.0
    )
    probs_low = to_low(probs)
    grad_probs = dot_last(grad_attn, key_value[:, head_size:])
    grad_scores = to_low(probs * (grad_probs - delta_rows[:, None]))
    grad_query = dot_plain(grad_scores, key_value[:, :head_size])
    grad_keys = dot_first(grad_scores, query_block) * score_scale
    grad_values = dot_first(probs_low, grad_attn)
    return (grad_query, jnp.concatenate([grad_keys, grad_values], axis=1))


def per_device(
    tokens,
    routes,
    lengths,
    cotangent,
    first_gain,
    first_shift,
    router,
    query_map,
    keyval,
    output_map,
    second_gain,
    second_shift,
    expand,
    expand_bias,
    contract,
    contract_bias,
):
    (
        gain_one,
        shift_one,
        router_weight,
        query_weight,
        keyval_weight,
        output_weight,
        gain_two,
        shift_two,
        expand_weight,
        expand_shift,
        contract_weight,
        contract_shift,
    ) = (
        lax.all_gather(to_low(first_gain), ("dp", "seq"), axis=0, tiled=True),
        lax.all_gather(to_low(first_shift), ("dp", "seq"), axis=0, tiled=True),
        lax.all_gather(to_low(router), ("dp", "seq"), axis=0, tiled=True),
        lax.all_gather(to_low(query_map), ("dp", "seq"), axis=0, tiled=True),
        lax.all_gather(to_low(keyval), ("dp", "seq"), axis=0, tiled=True),
        lax.all_gather(to_low(output_map), ("dp", "seq"), axis=0, tiled=True),
        lax.all_gather(to_low(second_gain), ("dp", "seq"), axis=0, tiled=True),
        lax.all_gather(to_low(second_shift), ("dp", "seq"), axis=0, tiled=True),
        lax.all_gather(to_low(expand), ("dp", "seq"), axis=0, tiled=True),
        lax.all_gather(to_low(expand_bias), ("dp", "seq"), axis=0, tiled=True),
        lax.all_gather(to_low(contract), ("dp", "seq"), axis=0, tiled=True),
        lax.all_gather(to_low(contract_bias), ("dp", "seq"), axis=0, tiled=True),
    )
    gain_one_f = gain_one.astype(jnp.float32)
    shift_one_f = shift_one.astype(jnp.float32)
    gain_two_f = gain_two.astype(jnp.float32)
    shift_two_f = shift_two.astype(jnp.float32)
    token_count = tokens.shape[0]
    expert_count = router_weight.shape[1]
    head_size = keyval_weight.shape[1] // 2
    choice_count = routes.shape[1]
    seq_count = lax.axis_size("seq")
    seq_length = token_count * seq_count
    score_scale = head_size ** (-0.5)
    key_rows = min(1024, seq_length)
    query_rows = token_count * choice_count
    block_rows = min(1024, query_rows)
    doc_ends = jnp.cumsum(lengths[0])
    positions = jnp.arange(seq_length, dtype=jnp.int32)
    doc_all = jnp.sum((positions[:, None] >= doc_ends[None, :]).astype(jnp.int32), axis=1)
    my_index = lax.axis_index("seq")
    doc_mine = lax.dynamic_slice_in_dim(doc_all, my_index * token_count, token_count, 0)
    doc_rows = jnp.repeat(doc_mine, choice_count)
    inputs = tokens.astype(jnp.float32)
    hidden = to_low(norm_rows(inputs, gain_one_f, shift_one_f))
    logits = dot_plain(hidden, router_weight)
    onehot = (
        routes[:, :, None] == jnp.arange(expert_count, dtype=jnp.int32)[None, None, :]
    ).astype(jnp.float32)
    picked = jnp.sum(logits[:, None, :] * onehot, axis=2)
    gate_weights = jax.nn.softmax(picked, axis=-1)
    query_all = dot_plain(hidden, query_weight).reshape(token_count, expert_count, head_size)
    queries = to_low(pick_rows(query_all, onehot)).reshape(query_rows, head_size)
    keyval_mine = to_low(dot_plain(hidden, keyval_weight))
    keyval_all = lax.all_gather(keyval_mine, "seq", axis=0, tiled=True)
    totals = []
    attn_parts = []
    for row_start in range(0, query_rows, block_rows):
        query_block = queries[row_start : row_start + block_rows]
        doc_block = doc_rows[row_start : row_start + block_rows]
        attn_block, log_total = attention_forward(
            query_block, doc_block, keyval_all, doc_all, key_rows, score_scale
        )
        totals.append(log_total)
        attn_parts.append(attn_block)
    log_totals = jnp.concatenate(totals, axis=0)
    attn_rows = jnp.concatenate(attn_parts, axis=0)
    attn_three = attn_rows.reshape(token_count, choice_count, head_size)
    mixed_heads = to_low(
        spread_rows(attn_three * gate_weights[:, :, None], onehot).reshape(
            token_count, expert_count * head_size
        )
    )
    middle = inputs + dot_plain(mixed_heads, output_weight)
    hidden_two = to_low(norm_rows(middle, gain_two_f, shift_two_f))
    inner_pre = dot_plain(hidden_two, expand_weight) + expand_shift.astype(jnp.float32)
    active = to_low(smooth_gate(inner_pre))
    result = middle + dot_plain(active, contract_weight) + contract_shift.astype(jnp.float32)
    layer_out = result.astype(jnp.bfloat16)
    grad_contract = dot_first(active, cotangent)
    grad_contract_bias = jnp.sum(cotangent.astype(jnp.float32), axis=0)
    grad_active = dot_last(cotangent, contract_weight)
    unused_gate, gate_back = jax.vjp(smooth_gate, inner_pre)
    grad_inner = to_low(gate_back(grad_active)[0])
    grad_expand = dot_first(hidden_two, grad_inner)
    grad_expand_bias = jnp.sum(grad_inner.astype(jnp.float32), axis=0)
    grad_hidden_two = dot_last(grad_inner, expand_weight)
    unused_norm, norm_back = jax.vjp(norm_rows, middle, gain_two_f, shift_two_f)
    grad_mid_norm, grad_second_gain, grad_second_shift = norm_back(grad_hidden_two)
    grad_middle = cotangent.astype(jnp.float32) + grad_mid_norm
    grad_branch = to_low(grad_middle)
    grad_output_map = dot_first(mixed_heads, grad_branch)
    grad_mixed = dot_last(grad_branch, output_weight).reshape(token_count, expert_count, head_size)
    grad_weighted = pick_rows(grad_mixed, onehot)
    grad_gates = jnp.sum(grad_weighted * attn_three, axis=-1)
    grad_attn = to_low(grad_weighted * gate_weights[:, :, None]).reshape(query_rows, head_size)
    grad_picked = gate_weights * (
        grad_gates - jnp.sum(gate_weights * grad_gates, axis=-1, keepdims=True)
    )
    grad_logits = to_low(jnp.sum(grad_picked[:, :, None] * onehot, axis=1))
    grad_router = dot_first(hidden, grad_logits)
    grad_hidden = dot_last(grad_logits, router_weight)
    delta_rows = jnp.sum(grad_attn.astype(jnp.float32) * attn_rows, axis=-1)
    block_starts = list(range(0, query_rows, block_rows))

    def key_step(block_index, carry):
        grad_kv_all, grad_query_all = carry
        offset = block_index * key_rows
        key_value = lax.dynamic_slice_in_dim(keyval_all, offset, key_rows, 0)
        doc_keys = lax.dynamic_slice_in_dim(doc_all, offset, key_rows, 0)
        query_parts = []
        kv_block = jnp.zeros((key_rows, 2 * head_size), jnp.float32)
        for row_start in block_starts:
            part_rows = slice(row_start, row_start + block_rows)
            grad_query, grad_kv_block = block_backward(
                queries[part_rows],
                doc_rows[part_rows],
                log_totals[part_rows],
                delta_rows[part_rows],
                grad_attn[part_rows],
                key_value,
                doc_keys,
                score_scale,
            )
            kv_block = kv_block + grad_kv_block
            query_parts.append(grad_query)
        grad_kv_all = lax.dynamic_update_slice_in_dim(grad_kv_all, kv_block, offset, 0)
        return (grad_kv_all, grad_query_all + jnp.concatenate(query_parts, axis=0))

    key_start = (
        jnp.zeros((seq_length, 2 * head_size), jnp.float32),
        jnp.zeros((query_rows, head_size), jnp.float32),
    )
    grad_kv_all, query_total = lax.fori_loop(0, seq_length // key_rows, key_step, key_start)
    grad_kv_mine = to_low(
        lax.psum_scatter(
            grad_kv_all.astype(jnp.bfloat16), "seq", scatter_dimension=0, tiled=True
        ).astype(jnp.float32)
    )
    grad_queries = to_low(query_total * score_scale).reshape(token_count, choice_count, head_size)
    placed = to_low(
        spread_rows(grad_queries.astype(jnp.float32), onehot).reshape(
            token_count, expert_count * head_size
        )
    )
    grad_query_map = dot_first(hidden, placed)
    grad_keyval = dot_first(hidden, grad_kv_mine)
    grad_hidden = (
        grad_hidden + dot_last(placed, query_weight) + dot_last(grad_kv_mine, keyval_weight)
    )
    unused_first, first_back = jax.vjp(norm_rows, inputs, gain_one_f, shift_one_f)
    grad_in_norm, grad_first_gain, grad_first_shift = first_back(grad_hidden)
    grad_tokens = (grad_middle + grad_in_norm).astype(jnp.bfloat16)
    every_sum = (
        lax.psum_scatter(grad_first_gain, ("dp", "seq"), scatter_dimension=0, tiled=True),
        lax.psum_scatter(grad_first_shift, ("dp", "seq"), scatter_dimension=0, tiled=True),
        lax.psum_scatter(grad_router, ("dp", "seq"), scatter_dimension=0, tiled=True),
        lax.psum_scatter(grad_query_map, ("dp", "seq"), scatter_dimension=0, tiled=True),
        lax.psum_scatter(grad_keyval, ("dp", "seq"), scatter_dimension=0, tiled=True),
        lax.psum_scatter(grad_output_map, ("dp", "seq"), scatter_dimension=0, tiled=True),
        lax.psum_scatter(grad_second_gain, ("dp", "seq"), scatter_dimension=0, tiled=True),
        lax.psum_scatter(grad_second_shift, ("dp", "seq"), scatter_dimension=0, tiled=True),
        lax.psum_scatter(grad_expand, ("dp", "seq"), scatter_dimension=0, tiled=True),
        lax.psum_scatter(grad_expand_bias, ("dp", "seq"), scatter_dimension=0, tiled=True),
        lax.psum_scatter(grad_contract, ("dp", "seq"), scatter_dimension=0, tiled=True),
        lax.psum_scatter(grad_contract_bias, ("dp", "seq"), scatter_dimension=0, tiled=True),
    )
    return (
        layer_out,
        grad_tokens,
        every_sum[0],
        every_sum[1],
        every_sum[2],
        every_sum[3],
        every_sum[4],
        every_sum[5],
        every_sum[6],
        every_sum[7],
        every_sum[8],
        every_sum[9],
        every_sum[10],
        every_sum[11],
    )


def solution(mesh):
    return jax.shard_map(
        per_device,
        mesh=mesh,
        in_specs=(
            P(("dp", "seq"), None),
            P(("dp", "seq"), None),
            P("dp", None),
            P(("dp", "seq"), None),
            P(("dp", "seq")),
            P(("dp", "seq")),
            P(("dp", "seq"), None),
            P(("dp", "seq"), None),
            P(("dp", "seq"), None),
            P(("dp", "seq"), None),
            P(("dp", "seq")),
            P(("dp", "seq")),
            P(("dp", "seq"), None),
            P(("dp", "seq")),
            P(("dp", "seq"), None),
            P(("dp", "seq")),
        ),
        out_specs=(
            P(("dp", "seq"), None),
            P(("dp", "seq"), None),
            P(("dp", "seq")),
            P(("dp", "seq")),
            P(("dp", "seq"), None),
            P(("dp", "seq"), None),
            P(("dp", "seq"), None),
            P(("dp", "seq"), None),
            P(("dp", "seq")),
            P(("dp", "seq")),
            P(("dp", "seq"), None),
            P(("dp", "seq")),
            P(("dp", "seq"), None),
            P(("dp", "seq")),
        ),
        check_vma=False,
    )
```

profile of v0, /device:TPU:0, one launch (start us, length us, event | category | flops | bytes accessed | tf_op | source)
XLA Modules:
  0.0 1373.9 jit_solution(12141934606836151029)
XLA Ops:
  13.2 42.2 %all-reduce.13 = (bf16[512]{0:T(512)(128)(2,1)S(1)}, bf16[512]{0:T(512)(128)(2,1)S(1)}, bf16[512]{0:T(512)(128)(2,1)S(1)}, bf16[512]{0:T(512)(128)(2,1)S(1)}, bf...) all-reduce(bf16[512]{0:T(512)(128)(2,1)S(1)} %dynamic-update-slice.1,, ...), channel_id=1, replica_groups=mesh['dp'=8,'seq'=4] {'dp','seq'}, use_global_device_ids=true, to_apply=%add.1 | all-reduce | flops 4608 | bytes 18432
  55.4 67.3 %all_gather.41 = bf16[512,128]{1,0:T(8,128)(2,1)S(1)} all-gather(bf16[16,128]{1,0:T(8,128)(2,1)S(1)} %convert_element_type.202), channel_id=1, replica_groups=mesh['dp'=8,'seq'=4] {'dp','seq'}, dimensions={0}, use_global_device_ids=true | all-gather | bytes 135168 | tf_op jit(solution)/shard_map/all_gather | solution.py:135
  128.2 70.6 %all_gather.43 = bf16[512,512]{1,0:T(8,128)(2,1)S(1)} all-gather(bf16[16,512]{1,0:T(8,128)(2,1)S(1)} %convert_element_type.204), channel_id=1, replica_groups=mesh['dp'=8,'seq'=4] {'dp','seq'}, dimensions={0}, use_global_device_ids=true | all-gather | bytes 540672 | tf_op jit(solution)/shard_map/all_gather | solution.py:134
  203.9 65.6 %all-gather = bf16[32,16,8]{1,2,0:T(8,128)(2,1)S(1)} all-gather(bf16[1,16,8]{1,2,0:T(8,128)(2,1)S(1)} %convert_bitcast_fusion), channel_id=1, replica_groups=mesh['dp'=8,'seq'=4] {'dp','seq'}, dimensions={0}, use_global_device_ids=true | all-gather | bytes 8448 | tf_op jit(solution)/shard_map/all_gather | solution.py:133
  271.1 73.8 %all_gather.45 = bf16[512,512]{1,0:T(8,128)(2,1)} all-gather(bf16[16,512]{1,0:T(8,128)(2,1)S(1)} %convert_element_type.210), channel_id=1, replica_groups=mesh['dp'=8,'seq'=4] {'dp','seq'}, dimensions={0}, use_global_device_ids=true | all-gather | bytes 540672 | tf_op jit(solution)/shard_map/all_gather | solution.py:136
  349.3 2.3 copy.130
  352.6 26.7 %while.52 = (s32[]{:T(128)}, f32[1024]{0:T(1024)S(1)}, f32[1024]{0:T(1024)S(1)}, f32[1024,64]{0,1:T(8,128)}, s32[4096]{0:T(1024)S(1)}, /*index=5*/bf16[4096,128]...) while((s32[]{:T(128)}, f32[1024]{0:T(1024)S(1)}, ...), condition=%wide.region_8.9_spmd.clone, body=%wide.region_5.0_spmd.clone.sunk | while | flops 285414400 | bytes 16103699 | solution.py:76
  356.4 2.2 fusion.218
  363.1 2.2 fusion.218
  369.7 2.2 fusion.218
  376.4 2.2 fusion.218
  379.3 23.4 %while.53 = (s32[]{:T(128)}, f32[1024]{0:T(1024)S(1)}, f32[1024]{0:T(1024)S(1)}, f32[1024,64]{0,1:T(8,128)S(1)}, s32[4096]{0:T(1024)S(1)}, /*index=5*/bf16[4096,...) while((s32[]{:T(128)}, f32[1024]{0:T(1024)S(1)}, ...), condition=%wide.region_12.13_spmd.clone, body=%wide.region_9.0_spmd.clone.sunk | while | flops 285414400 | bytes 13875419 | solution.py:76
  382.9 2.2 fusion.225
  388.8 2.2 fusion.225
  394.7 2.2 fusion.225
  400.5 2.2 fusion.225
  407.5 3.2 broadcast_multiply_fusion
  410.7 2.3 copy.128
  414.5 2.2 fusion.115
  418.4 11.4 multiply_convert_fusion
  429.8 10.7 convert_reduce_fusion
  440.5 4.2 fusion.116
  444.8 3.3 copy.131
  448.1 2.9 multiply_reduce_fusion.4
  455.2 2.3 copy.136
  460.8 45.9 %while.54 = (s32[]{:T(128)}, bf16[4096,128]{0,1:T(8,128)(2,1)}, f32[2048,64]{0,1:T(8,128)S(1)}, s32[2048]{0:T(1024)S(1)}, s32[4096]{0:T(1024)S(1)}, /*index=5*/b...) while((s32[]{:T(128)}, bf16[4096,128]{0,1:T(8,128)(2,1)}, ...), condition=%wide.region_27.28_spmd.clone, body=%wide.region_26.27_spmd.clone.sunk | while | flops 1372454912 | bytes 55673176 | solution.py:254
  463.2 1.8 fusion.253
  468.2 1.8 fusion.250
  474.6 1.8 fusion.253
  479.6 1.8 fusion.250
  486.1 1.8 fusion.253
  491.1 1.8 fusion.250
  497.5 1.8 fusion.253
  502.6 1.8 fusion.250
  510.8 3.0 fusion.121
  518.5 14.1 %reduce-scatter.10.cloned.1.call-done = bf16[1024,128]{0,1:T(8,128)(2,1)} async-done(((bf16[4096,128]{0,1:T(8,128)(2,1)}), bf16[1024,128]{0,1:T(8,128)(2,1)}) %reduce-scatter.10.cloned.1.call-update) | async-done | bytes 262160 | tf_op jit(solution)/shard_map/reduce_scatter | solution.py:256
  532.6 2.1 fusion.120
  534.8 6.5 fusion.122
  542.9 6.6 fusion.107
  550.1 5.2 add_convert_fusion.1
  558.1 109.2 %reduce-scatter.22.cloned.1.call-done = f32[16,8]{1,0:T(8,128)} async-done(((f32[512,8]{1,0:T(8,128)}), f32[16,8]{1,0:T(8,128)}) %reduce-scatter.22.cloned.1.call-update) | async-done | bytes 528
  669.1 2.7 fusion.109
  673.9 37.3 %all-reduce.12 = (f32[512]{0:T(512)S(1)}, f32[512]{0:T(512)S(1)}, f32[512]{0:T(512)S(1)}, f32[512]{0:T(512)S(1)}, f32[2048]{0:T(1024)S(1)}, /*index=5*/f32[512]{0:T(512)S(1)}) all-reduce(f32[512]{0:T(512)S(1)} %get-tuple-element.682, f32[512]{0:T(512)S(1)} %get-tuple-element.684, ...), channel_id=3, replica_groups=mesh['dp'=8,'seq'=4] {'dp','seq'}, use_global_device_ids=true, to_apply=%region_33.34.clone | all-reduce | flops 4608 | bytes 36864
  716.0 86.2 %reduce-scatter.16.cloned.1.call-done = f32[16,512]{1,0:T(8,128)} async-done(((f32[512,512]{1,0:T(8,128)}), f32[16,512]{1,0:T(8,128)}) %reduce-scatter.16.cloned.1.call-update) | async-done | bytes 32784 | tf_op jit(solution)/shard_map/reduce_scatter | solution.py:280
  802.2 134.8 %reduce-scatter.12.cloned.1.call-done = f32[16,512]{1,0:T(8,128)} async-done(((f32[512,512]{1,0:T(8,128)}), f32[16,512]{1,0:T(8,128)}) %reduce-scatter.12.cloned.1.call-update) | async-done | bytes 32784 | tf_op jit(solution)/shard_map/reduce_scatter | solution.py:278
  936.9 133.1 %reduce-scatter.14.cloned.1.call-done = f32[16,128]{1,0:T(8,128)} async-done(((f32[512,128]{1,0:T(8,128)}), f32[16,128]{1,0:T(8,128)}) %reduce-scatter.14.cloned.1.call-update) | async-done | bytes 8208 | tf_op jit(solution)/shard_map/reduce_scatter | solution.py:279
  1070.1 147.6 %reduce-scatter.20.cloned.1.call-done = f32[64,512]{1,0:T(8,128)} async-done(((f32[2048,512]{1,0:T(8,128)}), f32[64,512]{1,0:T(8,128)}) %reduce-scatter.20.cloned.1.call-update) | async-done | bytes 131088 | tf_op jit(solution)/shard_map/reduce_scatter | solution.py:285
  1217.7 149.2 %reduce-scatter.18.cloned.1.call-done = f32[16,2048]{1,0:T(8,128)} async-done(((f32[512,2048]{1,0:T(8,128)}), f32[16,2048]{1,0:T(8,128)}) %reduce-scatter.18.cloned.1.call-update) | async-done | bytes 131088 | tf_op jit(solution)/shard_map/reduce_scatter | solution.py:283
  (425 shorter events, 123.2 us)
Async XLA Ops:
  7.2 119.4 %copy-start.43 = (f32[16,2048]{1,0:T(8,128)S(1)}, f32[16,2048]{1,0:T(8,128)}, u32[]{:S(2)}) copy-start(f32[16,2048]{1,0:T(8,128)} %param.34) | copy-start | bytes 393220
  7.2 345.4 %all-gather.5.cloned.1.call-start = ((), (), s32[]{:S(2)}) async-start(), calls=%async_computation.7 | async-start | bytes 1310720 | tf_op jit(solution)/shard_map/all_gather | solution.py:175
  55.4 71.9 %copy-start.55 = (f32[512]{0:T(512)}, f32[512]{0:T(512)S(1)}, u32[]{:S(2)}) copy-start(f32[512]{0:T(512)S(1)} %convert_element_type.198) | copy-start | bytes 6148
  55.4 72.0 %copy-start.44 = (f32[64,512]{1,0:T(8,128)S(1)}, f32[64,512]{1,0:T(8,128)}, u32[]{:S(2)}) copy-start(f32[64,512]{1,0:T(8,128)} %param.36) | copy-start | bytes 393220
  122.7 5.3 copy-start.26
  122.7 5.4 copy-start.61
  122.7 5.5 copy-start.49
  124.3 290.2 %copy-start = (bf16[1024,512]{0,1:T(8,128)(2,1)}, bf16[1024,512]{0,1:T(8,128)(2,1)S(1)}, u32[]{:S(2)}) copy-start(bf16[1024,512]{0,1:T(8,128)(2,1)S(1)} %copy.122) | copy-start | bytes 3145732
  124.8 74.8 %copy-start.59 = (f32[1024]{0:T(1024)}, f32[1024]{0:T(1024)S(1)}, u32[]{:S(2)}) copy-start(f32[1024]{0:T(1024)S(1)} %fusion.93) | copy-start | bytes 12292
  124.8 74.8 %copy-start.51 = (f32[1024]{0:T(1024)}, f32[1024]{0:T(1024)S(1)}, u32[]{:S(2)}) copy-start(f32[1024]{0:T(1024)S(1)} %fusion.105) | copy-start | bytes 12292
  125.3 222.0 %copy-start.2 = (bf16[1024,512]{0,1:T(8,128)(2,1)}, bf16[1024,512]{0,1:T(8,128)(2,1)S(1)}, u32[]{:S(2)}) copy-start(bf16[1024,512]{0,1:T(8,128)(2,1)S(1)} %fusion.91) | copy-start | bytes 3145732
  126.5 291.8 %all-gather.7.cloned.1.call-start = ((), (), s32[]{:S(2)}) async-start(), calls=%async_computation.8 | async-start | bytes 2162688 | tf_op jit(solution)/shard_map/all_gather | solution.py:139
  127.3 73.8 %copy-start.71 = (s32[1,13]{1,0:T(1,128)S(1)}, s32[1,13]{1,0:T(1,128)}, u32[]{:S(2)}) copy-start(s32[1,13]{1,0:T(1,128)} %param.24) | copy-start | bytes 160
  127.3 74.0 %copy-start.66 = (f32[16,8]{0,1:T(8,128)S(1)}, f32[16,8]{0,1:T(8,128)}, u32[]{:S(2)}) copy-start(f32[16,8]{0,1:T(8,128)} %param.28) | copy-start | bytes 1540
  127.3 302.5 %all-gather.9.cloned.1.call-start = ((), (), s32[]{:S(2)}) async-start(), calls=%async_computation.9 | async-start | bytes 2162688 | tf_op jit(solution)/shard_map/all_gather | solution.py:141
  128.0 404.5 %reduce-scatter.10.cloned.1.call-start = ((), (), s32[]{:S(2)}) async-start(), calls=%async_computation.10 | async-start | bytes 1310720 | tf_op jit(solution)/shard_map/reduce_scatter | solution.py:256
  201.0 150.5 %copy-start.33 = (bf16[512,2,64]{0,2,1:T(8,128)(2,1)S(1)}, bf16[512,2,64]{0,2,1:T(8,128)(2,1)}, u32[]{:S(2)}) copy-start(bf16[512,2,64]{0,2,1:T(8,128)(2,1)} %get-tuple-element.770) | copy-start | bytes 393220
  201.0 151.3 %copy-start.32 = (bf16[512,2,64]{0,2,1:T(8,128)(2,1)S(1)}, bf16[512,2,64]{0,2,1:T(8,128)(2,1)}, u32[]{:S(2)}) copy-start(bf16[512,2,64]{0,2,1:T(8,128)(2,1)} %get-tuple-element.771) | copy-start | bytes 393220
  271.1 81.5 %copy-start.47 = (bf16[512,8]{0,1:T(8,128)(2,1)}, bf16[512,8]{0,1:T(8,128)(2,1)S(1)}, u32[]{:S(2)}) copy-start(bf16[512,8]{0,1:T(8,128)(2,1)S(1)} %reshape.321) | copy-start | bytes 24580
  352.6 26.7 %copy-start.36 = (f32[1024,64]{0,1:T(8,128)S(1)}, f32[1024,64]{0,1:T(8,128)}, u32[]{:S(2)}) copy-start(f32[1024,64]{0,1:T(8,128)} %custom-call.5) | copy-start | bytes 786436
  407.5 9.2 copy-start.13
  413.0 5.4 copy-start.62
  413.0 5.4 copy-start.64
  418.3 11.5 copy-start.28
  429.8 10.7 copy-start.70
  440.5 4.2 copy-start.72
  452.6 4.9 copy-start.25
  453.6 7.2 copy-start.7
  453.9 6.8 copy-start.16
  460.8 48.7 %copy-start.35 = (f32[1024,2]{0,1:T(2,128)S(1)}, f32[1024,2]{0,1:T(2,128)}, u32[]{:S(2)}) copy-start(f32[1024,2]{0,1:T(2,128)} %copy-done.34) | copy-start | bytes 24580
  460.8 48.7 %copy-start.46 = (f32[1024]{0:T(1024)S(1)}, f32[1024]{0:T(1024)}, u32[]{:S(2)}) copy-start(f32[1024]{0:T(1024)} %copy-done.45) | copy-start | bytes 12292
  460.8 48.7 %copy-start.54 = (f32[1024]{0:T(1024)S(1)}, f32[1024]{0:T(1024)}, u32[]{:S(2)}) copy-start(f32[1024]{0:T(1024)} %copy-done.53) | copy-start | bytes 12292
  460.8 48.8 %copy-start.50 = (s32[1024,2]{0,1:T(2,128)S(1)}, s32[1024,2]{0,1:T(2,128)}, u32[]{:S(2)}) copy-start(s32[1024,2]{0,1:T(2,128)} %param.23) | copy-start | bytes 24580
  460.8 48.8 %copy-start.3 = (bf16[1024,512]{0,1:T(8,128)(2,1)S(1)}, bf16[1024,512]{0,1:T(8,128)(2,1)}, u32[]{:S(2)}) copy-start(bf16[1024,512]{0,1:T(8,128)(2,1)} %copy-done.2) | copy-start | bytes 3145732
  506.8 160.5 %reduce-scatter.22.cloned.1.call-start = ((), (), s32[]{:S(2)}) async-start(), calls=%async_computation.16 | async-start | bytes 270336
  509.6 4.7 copy-start.42
  510.8 291.4 %reduce-scatter.16.cloned.1.call-start = ((), (), s32[]{:S(2)}) async-start(), calls=%async_computation.13 | async-start | bytes 1081344 | tf_op jit(solution)/shard_map/reduce_scatter | solution.py:280
  513.9 423.1 %reduce-scatter.12.cloned.1.call-start = ((), (), s32[]{:S(2)}) async-start(), calls=%async_computation.11 | async-start | bytes 1081344 | tf_op jit(solution)/shard_map/reduce_scatter | solution.py:278
  515.2 19.5 %copy-start.29 = (bf16[1024,512]{1,0:T(8,128)(2,1)S(1)}, bf16[1024,512]{1,0:T(8,128)(2,1)}, u32[]{:S(2)}) copy-start(bf16[1024,512]{1,0:T(8,128)(2,1)} %param.25) | copy-start | bytes 3145732
  518.5 551.6 %reduce-scatter.14.cloned.1.call-start = ((), (), s32[]{:S(2)}) async-start(), calls=%async_computation.12 | async-start | bytes 270336 | tf_op jit(solution)/shard_map/reduce_scatter | solution.py:279
  534.7 683.0 %reduce-scatter.20.cloned.1.call-start = ((), (), s32[]{:S(2)}) async-start(), calls=%async_computation.15 | async-start | bytes 4325376 | tf_op jit(solution)/shard_map/reduce_scatter | solution.py:285
  541.3 825.6 %reduce-scatter.18.cloned.1.call-start = ((), (), s32[]{:S(2)}) async-start(), calls=%async_computation.14 | async-start | bytes 4325376 | tf_op jit(solution)/shard_map/reduce_scatter | solution.py:283
  550.1 6.8 copy-start.48
  555.3 113.3 %copy-start.27 = (bf16[512,128]{1,0:T(8,128)(2,1)S(1)}, bf16[512,128]{1,0:T(8,128)(2,1)}, u32[]{:S(2)}) copy-start(bf16[512,128]{1,0:T(8,128)(2,1)} %copy-done.26) | copy-start | bytes 393220
  555.4 113.3 %copy-start.30 = (bf16[1024,128]{0,1:T(8,128)(2,1)S(1)}, bf16[1024,128]{0,1:T(8,128)(2,1)}, u32[]{:S(2)}) copy-start(bf16[1024,128]{0,1:T(8,128)(2,1)} %reduce-scatter.10.cloned.1.call-done) | copy-start | bytes 786436
  555.4 113.7 %copy-start.1 = (bf16[1024,512]{0,1:T(8,128)(2,1)S(1)}, bf16[1024,512]{0,1:T(8,128)(2,1)}, u32[]{:S(2)}) copy-start(bf16[1024,512]{0,1:T(8,128)(2,1)} %copy-done) | copy-start | bytes 3145732
  555.4 113.7 %copy-start.41 = (f32[1024]{0:T(1024)S(1)}, f32[1024]{0:T(1024)}, u32[]{:S(2)}) copy-start(f32[1024]{0:T(1024)} %copy-done.40) | copy-start | bytes 12292
  555.4 113.7 %copy-start.56 = (f32[512]{0:T(512)S(1)}, f32[512]{0:T(512)}, u32[]{:S(2)}) copy-start(f32[512]{0:T(512)} %copy-done.55) | copy-start | bytes 6148
  (50 other events, 89.7 us)
Sparse Core Ops, SparseCore 0:
  126.6 28.1 all-gather.4
  157.8 55.7 all-gather.6
  216.5 55.4 all-gather.8
  506.9 25.6 reduce-scatter.9
  534.8 132.4 reduce-scatter.21
  670.0 132.1 reduce-scatter.15
  805.1 131.8 reduce-scatter.11
  939.7 130.2 reduce-scatter.13
  1073.0 144.6 reduce-scatter.19
  1220.5 146.3 reduce-scatter.17
where the time goes:
time: 1380 us; the launch traced here: 1370 us
  waiting for transfers between devices  774 us (56%)
  blocking collectives  357 us (26%)
  matrix products  134 us (10%)
  local copies, waits for them, and re-layouts  52.5 us (4%)
  other arithmetic  39.3 us (3%)
  between operations  15.5 us (1%)
    reduce_scatter x1, waiting for transfers between devices, per_device(): lax.psum_scatter(grad_expand, ('dp', 'seq'), scatter_dimension=0, tiled=T...  149 us
    reduce_scatter x1, waiting for transfers between devices, per_device(): lax.psum_scatter(grad_contract, ('dp', 'seq'), scatter_dimension=0, tiled...  148 us
    reduce_scatter x1, waiting for transfers between devices, per_device(): lax.psum_scatter(grad_query_map, ('dp', 'seq'), scatter_dimension=0, tile...  135 us
    reduce_scatter x1, waiting for transfers between devices, per_device(): lax.psum_scatter(grad_keyval, ('dp', 'seq'), scatter_dimension=0, tiled=T...  133 us
    unnamed x11, waiting for transfers between devices  109 us
    reduce_scatter x1, waiting for transfers between devices, per_device(): lax.psum_scatter(grad_output_map, ('dp', 'seq'), scatter_dimension=0, til...  86.2 us
    unnamed x2, blocking collectives  79.4 us
    all_gather x1, blocking collectives, per_device(): lax.all_gather(to_low(output_map), ('dp', 'seq'), axis=0, tiled=True)  73.8 us
  transfers between devices with their start and end apart: 10, of which 7 were waited for; matrix products, arithmetic and copies ran while one was open for 9% of the time, Pallas kernels for 0%

commit v1 on v0

v1 whole, which is shorter than its diff:
```python
import functools

import jax
import jax.numpy as jnp
from jax import lax
from jax.experimental import pallas as pl
from jax.experimental.pallas import tpu as pltpu
from jax.sharding import PartitionSpec as P

LOW = jnp.bfloat16
FULL = jnp.float32
FAR = 1e30
EPS = 1e-05
DOC_LANE = 64
LSE_LANE = 96
SUM_LANE = 64
MAX_LANE = 67
LANES = 128
MEGA = 1 << 20


def to_low(matrix):
    return matrix.astype(LOW)


def dot_plain(left, right):
    return lax.dot_general(left, right, (((1,), (0,)), ((), ())), preferred_element_type=FULL)


def dot_last(left, right):
    return lax.dot_general(left, right, (((1,), (1,)), ((), ())), preferred_element_type=FULL)


def dot_first(left, right):
    return lax.dot_general(left, right, (((0,), (0,)), ((), ())), preferred_element_type=FULL)


def index_bits(axis):
    size = lax.axis_size(axis)
    return [(axis, 1 << b) for b in range(size.bit_length() - 1)]


def bit_of(stage):
    axis, mask = stage
    return (lax.axis_index(axis) & mask) // mask


def exchange(block, stage):
    axis, mask = stage
    pairs = [(i, i ^ mask) for i in range(lax.axis_size(axis))]
    return lax.ppermute(block, axis, pairs)


def device_bits():
    return index_bits("dp")[::-1] + index_bits("seq")[::-1]


def stage_orders():
    dp_bits, seq_bits = index_bits("dp"), index_bits("seq")
    core, plane = dp_bits[:1], dp_bits[1:]
    return (seq_bits + plane + core, seq_bits + plane[::-1] + core)


def gather_blocks(block, stages):
    order = device_bits()
    have = []
    lead, tail = block.shape[0], block.shape[1:]
    for stage in stages:
        other = exchange(block, stage)
        position = 1 + sum(1 for s in have if order.index(s) < order.index(stage))
        swap = bit_of(stage) == 1
        first = jnp.where(swap, other, block)
        second = jnp.where(swap, block, other)
        block = jnp.stack([first, second], axis=position)
        have.append(stage)
    return block.reshape(lead, -1, tail[1])


def scatter_sum(blocks, stages):
    order = device_bits()
    left = list(order)
    lead, total, columns = blocks.shape
    value = blocks.reshape((lead,) + (2,) * len(order) + (total >> len(order), columns))
    for stage in stages:
        position = 1 + left.index(stage)
        bit = bit_of(stage)
        keep = lax.dynamic_index_in_dim(value, bit, position, keepdims=False)
        send = lax.dynamic_index_in_dim(value, 1 - bit, position, keepdims=False)
        value = keep.astype(FULL) + exchange(to_low(send), stage).astype(FULL)
        left.remove(stage)
    return value


def lane_ids(shape):
    return lax.broadcasted_iota(jnp.int32, shape, len(shape) - 1)


def row_positions(offset, rows):
    return offset + lax.broadcasted_iota(jnp.int32, (rows, 1), 0)


def in_document(bounds_ref, positions):
    return (positions >= bounds_ref[0:1, :]) & (positions < bounds_ref[1:2, :])


def three_parts(column):
    first = to_low(column).astype(FULL)
    rest = column - first
    second = to_low(rest).astype(FULL)
    return first, second, rest - second


def put_parts(base, lanes, lane, column):
    for step, part in enumerate(three_parts(column)):
        base = jnp.where(lanes == lane + step, part, base)
    return base


def normalize(matrix):
    center = matrix - jnp.mean(matrix, axis=1, keepdims=True)
    spread = jnp.mean(center * center, axis=1, keepdims=True)
    factor = lax.rsqrt(spread + EPS)
    return center * factor, factor


def norm_backward(grad, unit, factor, gain):
    scaled = grad * gain
    mean = jnp.mean(scaled, axis=1, keepdims=True)
    along = jnp.mean(scaled * unit, axis=1, keepdims=True)
    return factor * (scaled - mean - unit * along)


def half_of(route, head):
    return route % (LANES // head)


def choose(wide, route, head):
    per_tile = LANES // head
    tile = route // per_tile
    picked = wide[:, :LANES]
    for index in range(1, wide.shape[1] // LANES):
        picked = jnp.where(tile == index, wide[:, index * LANES : (index + 1) * LANES], picked)
    turned = pltpu.roll(picked, head, 1)
    lanes = lane_ids((1, LANES))
    mine = (lanes // head) == (route % per_tile)
    return jnp.where(mine, picked, turned)


def place(doubled, routes, head, width):
    lanes = lane_ids((1, LANES))
    per_tile = LANES // head
    tiles = []
    for index in range(width // LANES):
        expert = lanes // head + index * per_tile
        tile = jnp.zeros_like(doubled[0])
        for rows, route in zip(doubled, routes):
            tile = jnp.where(expert == route, rows, tile)
        tiles.append(tile)
    return jnp.concatenate(tiles, axis=1)


def doubled_head(rows, head):
    lanes = lane_ids((1, LANES))
    return jnp.where(lanes < head, rows, pltpu.roll(rows, head, 1))


def key_rows_of(kv, hot, head):
    lanes = lane_ids((1, LANES))
    kv = kv.astype(FULL)
    marks = jnp.where((lanes >= LSE_LANE) & (lanes < LSE_LANE + 3), 1.0, 0.0)
    keys = jnp.where(lanes < head, kv, jnp.where(hot, 1.0, marks))
    ones = jnp.where((lanes >= SUM_LANE) & (lanes < SUM_LANE + 3), 1.0, 0.0)
    values = jnp.where(lanes < head, pltpu.roll(kv, head, 1), ones)
    return to_low(keys), to_low(values)


def hidden_kernel(tokens_ref, side_ref, routes_ref, hidden_ref, kv_ref, gates_ref, *, experts):
    side = side_ref[...]
    vectors = side[:, LANES:].astype(FULL).T
    unit, factor = normalize(tokens_ref[...].astype(FULL))
    hidden = to_low(unit * vectors[experts : experts + 1] + vectors[experts + 1 : experts + 2])
    hidden_ref[...] = hidden
    both = dot_plain(hidden, side)
    kv_ref[...] = to_low(both[:, :LANES])
    logits = both[:, LANES:]
    lanes = lane_ids((1, LANES))
    picked = [
        jnp.sum(jnp.where(lanes == routes_ref[:, j : j + 1], logits, 0.0), axis=1, keepdims=True)
        for j in range(2)
    ]
    top = jnp.maximum(picked[0], picked[1])
    raised = [jnp.exp(p - top) for p in picked]
    total = raised[0] + raised[1]
    gates_ref[...] = jnp.where(
        lanes == 0, raised[0] / total, jnp.where(lanes == 1, raised[1] / total, 0.0)
    )


def query_kernel(
    place_ref, hidden_ref, weight_ref, routes_ref, bounds_ref, query_ref, *, head, rows
):
    wide = dot_plain(hidden_ref[...], weight_ref[...])
    lanes = lane_ids((1, LANES))
    hot = in_document(bounds_ref, row_positions(place_ref[0] + pl.program_id(0) * rows, rows))
    documents = (bounds_ref[1:2, :] > 0) & (lanes >= head)
    marks = jnp.where(documents & jnp.logical_not(hot), -FAR, 0.0)
    for j in range(2):
        rows_of = choose(wide, routes_ref[:, j : j + 1], head) * head**-0.5
        query_ref[j] = to_low(jnp.where(lanes < head, rows_of, marks))


def forward_kernel(place_ref, query_ref, kv_ref, bounds_ref, *rest, head, first, last):
    rest = list(rest)
    state_ref = None if first else rest.pop(0)
    if last:
        attn_ref, wide_ref, held = rest
    else:
        held_ref, held = rest
    step = pl.program_id(1)
    query = query_ref[...]
    rows = query.shape[0]
    key_count = kv_ref.shape[0]
    lanes = lane_ids((1, LANES))
    hot = in_document(bounds_ref, row_positions(place_ref[step], key_count))
    keys, values = key_rows_of(kv_ref[...], hot, head)
    scores = dot_last(query, keys)
    top = jnp.max(scores, axis=1, keepdims=True)

    @pl.when(step == 0)
    def _():
        if first:
            held[...] = jnp.where(lanes == MAX_LANE, -FAR, jnp.zeros((rows, LANES), FULL))
        else:
            held[...] = state_ref[...]

    before = held[...]
    old = before[:, MAX_LANE : MAX_LANE + 1]
    new = jnp.maximum(old, top)
    weights = to_low(jnp.exp(scores - new))
    after = before * jnp.exp(old - new) + dot_plain(weights, values)
    held[...] = jnp.where(lanes == MAX_LANE, new, after)

    @pl.when(step == pl.num_programs(1) - 1)
    def _():
        end = held[...]
        if last:
            total = end[:, SUM_LANE : SUM_LANE + 1]
            attn_ref[...] = jnp.where(lanes < head, end / total, 0.0)
            log_total = end[:, MAX_LANE : MAX_LANE + 1] + jnp.log(total)
            wide_ref[...] = to_low(
                put_parts(query_ref[...].astype(FULL), lanes, LSE_LANE, -log_total)
            )
        else:
            held_ref[...] = end


def middle_kernel(
    tokens_ref,
    cotangent_ref,
    attn_ref,
    gates_ref,
    routes_ref,
    vectors_ref,
    bias_ref,
    pair_ref,
    contract_ref,
    out_ref,
    grad_middle_ref,
    grad_attn_ref,
    grad_logits_ref,
    grad_pair_ref,
    grad_contract_ref,
    grad_rows_ref,
    grad_bias_ref,
    pair_sum,
    contract_sum,
    *,
    head,
):
    step = pl.program_id(0)

    @pl.when(step == 0)
    def _():
        pair_sum[...] = jnp.zeros_like(pair_sum)
        contract_sum[...] = jnp.zeros_like(contract_sum)
        grad_rows_ref[...] = jnp.zeros_like(grad_rows_ref)
        grad_bias_ref[...] = jnp.zeros_like(grad_bias_ref)

    width = tokens_ref.shape[1]
    chunks = pair_ref.shape[0] - 1
    part = contract_ref.shape[0] // chunks
    gain, shift, contract_bias = (vectors_ref[i : i + 1, :] for i in range(3))
    lanes = lane_ids((1, LANES))
    routes = [routes_ref[:, j : j + 1] for j in range(2)]
    gates = [gates_ref[:, j : j + 1] for j in range(2)]
    attn = [attn_ref[j] for j in range(2)]
    mixed = to_low(
        place([doubled_head(a, head) * g for a, g in zip(attn, gates)], routes, head, width)
    )
    middle = tokens_ref[...].astype(FULL) + dot_plain(mixed, pair_ref[0])
    unit, factor = normalize(middle)
    hidden = to_low(unit * gain + shift)
    cotangent = cotangent_ref[...]
    cotangent_full = cotangent.astype(FULL)
    out = middle + contract_bias
    grad_hidden = jnp.zeros_like(middle)
    slope = 0.7978845608028654
    cube = 0.044715
    for chunk in range(chunks):
        rows = pl.ds(chunk * part, part)
        expand = pair_ref[chunk + 1]
        contract = contract_ref[rows, :]
        inner = dot_plain(hidden, expand) + bias_ref[:, rows]
        square = inner * inner
        bent = jnp.tanh(slope * inner * (1.0 + cube * square))
        half = 0.5 * (1.0 + bent)
        active = to_low(inner * half)
        out += dot_plain(active, contract)
        steep = half + 0.5 * inner * (1.0 - bent * bent) * (slope + 3.0 * cube * slope * square)
        grad_inner_full = steep * dot_last(cotangent, contract)
        grad_inner = to_low(grad_inner_full)
        grad_bias_ref[0:1, rows] += jnp.sum(grad_inner.astype(FULL), axis=0, keepdims=True)
        contract_sum[rows, :] += dot_first(active, cotangent)
        pair_sum[chunk + 1] += dot_first(hidden, grad_inner)
        grad_hidden += dot_last(grad_inner, expand)
    out_ref[...] = to_low(out)
    grad_middle = cotangent_full + norm_backward(grad_hidden, unit, factor, gain)
    grad_middle_ref[...] = grad_middle
    grad_rows_ref[0:1, :] += jnp.sum(grad_hidden * unit, axis=0, keepdims=True)
    grad_rows_ref[1:2, :] += jnp.sum(grad_hidden, axis=0, keepdims=True)
    grad_rows_ref[2:3, :] += jnp.sum(cotangent_full, axis=0, keepdims=True)
    branch = to_low(grad_middle)
    pair_sum[0] += dot_first(mixed, branch)
    grad_mixed = dot_last(branch, pair_ref[0])
    grad_gates = []
    for j in range(2):
        weighted = jnp.where(lanes < head, choose(grad_mixed, routes[j], head), 0.0)
        grad_gates.append(jnp.sum(weighted * attn[j], axis=1, keepdims=True))
        grad_attn = to_low(weighted * gates[j]).astype(FULL)
        delta = jnp.sum(grad_attn * attn[j], axis=1, keepdims=True)
        grad_attn_ref[j] = to_low(put_parts(grad_attn, lanes, SUM_LANE, -delta))
    mean = gates[0] * grad_gates[0] + gates[1] * grad_gates[1]
    grad_logits = jnp.zeros(gates_ref.shape, FULL)
    for j in range(2):
        grad_logits = jnp.where(lanes == routes[j], gates[j] * (grad_gates[j] - mean), grad_logits)
    grad_logits_ref[...] = to_low(grad_logits)

    @pl.when(step == pl.num_programs(0) - 1)
    def _():
        grad_pair_ref[...] = to_low(pair_sum[...])
        grad_contract_ref[...] = to_low(contract_sum[...])


def backward_kernel(
    place_ref, query_ref, grad_ref, kv_ref, bounds_ref, *rest, head, first, rows
):
    rest = list(rest)
    before_ref = None if first else rest.pop(0)
    grad_query_ref, grad_kv_ref, total = rest
    block, step = pl.program_id(0), pl.program_id(1)
    lanes = lane_ids((1, LANES))
    key_count = kv_ref.shape[0]
    hot = in_document(bounds_ref, row_positions(place_ref[block], key_count))
    keys, values = key_rows_of(kv_ref[...], hot, head)
    query = query_ref[...]
    grad = grad_ref[...]
    probs = jnp.exp(dot_last(keys, query))
    grad_scores = to_low(probs * dot_last(values, grad))
    only_query = to_low(jnp.where(lanes < head, query.astype(FULL), 0.0))
    turned = pltpu.roll(grad.astype(FULL), head, 1)
    only_grad = to_low(jnp.where(lanes < head, 0.0, turned))
    update = dot_plain(grad_scores, only_query) + dot_plain(to_low(probs), only_grad)

    @pl.when(step == 0)
    def _():
        total[...] = update

    @pl.when(step > 0)
    def _():
        total[...] += update

    @pl.when(step == pl.num_programs(1) - 1)
    def _():
        grad_kv_ref[...] = to_low(total[...])

    here = pl.ds(pl.multiple_of(step * rows, rows), rows)
    grad_query = dot_first(grad_scores, keys)

    @pl.when(block == 0)
    def _():
        if first:
            grad_query_ref[here, :] = grad_query
        else:
            grad_query_ref[here, :] = before_ref[here, :] + grad_query

    @pl.when(block > 0)
    def _():
        grad_query_ref[here, :] += grad_query


def placed_kernel(
    grad_query_ref, hidden_ref, routes_ref, grad_logits_ref, weight_ref, side_ref,
    grad_hidden_ref, grad_weight_ref, grad_router_ref, total, router_total, *, head
):
    step = pl.program_id(0)

    @pl.when(step == 0)
    def _():
        total[...] = jnp.zeros_like(total)
        router_total[...] = jnp.zeros_like(router_total)

    width = hidden_ref.shape[1]
    lanes = lane_ids((1, LANES))
    rows = [
        doubled_head(to_low(grad_query_ref[j] * head**-0.5).astype(FULL), head) for j in range(2)
    ]
    placed = to_low(place(rows, [routes_ref[:, j : j + 1] for j in range(2)], head, width))
    hidden = hidden_ref[...]
    grad_logits = grad_logits_ref[...]
    total[...] += dot_first(hidden, placed)
    router_total[...] += dot_first(hidden, grad_logits)
    grad_hidden_ref[...] = dot_last(placed, weight_ref[...]) + dot_last(
        grad_logits, side_ref[:, LANES:]
    )

    @pl.when(step == pl.num_programs(0) - 1)
    def _():
        grad_weight_ref[...] = to_low(total[...])
        grad_router_ref[...] = router_total[...]


def last_kernel(
    tokens_ref, hidden_ref, grad_hidden_ref, grad_middle_ref, side_ref, rows_ref, grad_router_ref,
    own_ref, *rest, experts, others
):
    other_refs = rest[:others]
    grad_tokens_ref, grad_side_ref, total, sums = rest[others:]
    step = pl.program_id(0)

    @pl.when(step == 0)
    def _():
        total[...] = jnp.zeros_like(total)
        sums[...] = jnp.zeros_like(sums)

    side = side_ref[...]
    gain = side[:, LANES:].astype(FULL).T[experts : experts + 1]
    grad_kv = own_ref[...].astype(FULL)
    for ref in other_refs:
        grad_kv += ref[...].astype(FULL)
    grad_kv = to_low(grad_kv)
    total[...] += dot_first(hidden_ref[...], grad_kv)
    grad_hidden = grad_hidden_ref[...] + dot_last(grad_kv, side[:, :LANES])
    unit, factor = normalize(tokens_ref[...].astype(FULL))
    grad_tokens_ref[...] = to_low(
        grad_middle_ref[...] + norm_backward(grad_hidden, unit, factor, gain)
    )
    sums[0:1, :] += jnp.sum(grad_hidden * unit, axis=0, keepdims=True)
    sums[1:2, :] += jnp.sum(grad_hidden, axis=0, keepdims=True)

    @pl.when(step == pl.num_programs(0) - 1)
    def _():
        width = sums.shape[1]
        ahead = jnp.zeros((experts, width), FULL)
        behind = jnp.zeros((LANES - experts - 8, width), FULL)
        rows = lax.broadcasted_iota(jnp.int32, (8, 1), 0)
        vectors = jnp.where(rows < 2, sums[...], rows_ref[...])
        columns = jnp.concatenate([ahead, vectors, behind], axis=0).T
        grad_side_ref[:, :LANES] = to_low(total[...])
        grad_side_ref[:, LANES:] = to_low(columns + grad_router_ref[...])


def whole_spec(shape):
    return pl.BlockSpec(tuple(shape), lambda *ids: (0,) * len(shape))


def smem_spec():
    return pl.BlockSpec(memory_space=pltpu.SMEM)


def call(kernel, name, grid, in_specs, out_specs, out_shape, scratch=(), flops=0, moved=0):
    return pl.pallas_call(
        kernel,
        grid=grid,
        in_specs=in_specs,
        out_specs=out_specs,
        out_shape=out_shape,
        scratch_shapes=list(scratch),
        compiler_params=pltpu.CompilerParams(
            dimension_semantics=("arbitrary",) * len(grid), vmem_limit_bytes=48 * MEGA
        ),
        cost_estimate=pl.CostEstimate(flops=flops, bytes_accessed=moved, transcendentals=0),
        name=name,
    )


def shape_of(shape, dtype):
    return jax.ShapeDtypeStruct(tuple(shape), dtype)


def mask_groups(seq_count, first_masks):
    rest = [m for m in range(1, seq_count) if m not in first_masks]
    order = [m for m in first_masks if m < seq_count] + rest
    size = max(1, -(-len(order) // 3))
    return [order[i : i + size] for i in range(0, len(order), size)]


def per_device(
    tokens, routes, lengths, cotangent, first_gain, first_shift, router, query_map, keyval,
    output_map, second_gain, second_shift, expand, expand_bias, contract, contract_bias
):
    order_a, order_b = stage_orders()
    token_count, width = tokens.shape
    rows = first_gain.shape[0]
    experts = router.shape[1]
    head = keyval.shape[1] // 2
    inner_width = expand.shape[1]
    chunks = inner_width // width
    seq_count = lax.axis_size("seq")
    my_index = lax.axis_index("seq")

    columns = [first_gain, first_shift, second_gain, second_shift, contract_bias]
    extra = expand_bias.shape[0] // rows
    used = experts + len(columns) + extra
    side_mine = jnp.concatenate(
        [keyval, router]
        + [c[:, None] for c in columns]
        + [expand_bias.reshape(rows, extra), jnp.zeros((rows, LANES - used), FULL)],
        axis=1,
    )
    small_mine = to_low(jnp.concatenate([query_map, side_mine], axis=1))
    small_all = gather_blocks(small_mine[None], order_a)[0]
    query_weight = small_all[:, :width]
    side = small_all[:, width:]
    pair_mine = to_low(
        jnp.stack([output_map] + [expand[:, c * width : (c + 1) * width] for c in range(chunks)])
    )
    pair = gather_blocks(pair_mine, order_a)
    contract_all = gather_blocks(to_low(contract)[None], order_b)[0]
    vector_columns = side[:, LANES + experts + 2 : LANES + used].astype(FULL)
    vectors = jnp.pad(vector_columns[:, :3].T, ((0, 5), (0, 0)))
    bias = vector_columns[:, 3:].reshape(1, inner_width)

    ends = jnp.cumsum(lengths[0])
    starts = ends - lengths[0]
    count = ends.shape[0]
    fill = (DOC_LANE, LANES - DOC_LANE - count)
    bounds = jnp.pad(
        jnp.stack([jnp.pad(starts, fill, constant_values=1 << 30), jnp.pad(ends, fill)]),
        ((0, 6), (0, 0)),
    ).astype(jnp.int32)

    block = min(256, token_count)
    steps = token_count // block
    row_block = lambda n: pl.BlockSpec((block, n), lambda i: (i, 0))
    two_block = pl.BlockSpec((2, block, LANES), lambda i: (0, i, 0))
    side_width = side.shape[1]
    hidden, kv_mine, gates = call(
        functools.partial(hidden_kernel, experts=experts),
        "hidden",
        (steps,),
        [row_block(width), whole_spec(side.shape), row_block(2)],
        [row_block(width), row_block(LANES), row_block(LANES)],
        [
            shape_of((token_count, width), LOW),
            shape_of((token_count, LANES), LOW),
            shape_of((token_count, LANES), FULL),
        ],
        flops=2 * token_count * width * side_width,
        moved=4 * token_count * width,
    )(tokens, side, routes)

    def place_of(masks):
        return jnp.stack([(my_index ^ m) * token_count for m in masks]).astype(jnp.int32)

    shards = {0: kv_mine}
    for mask in list(range(2, seq_count)) + [1]:
        if mask < seq_count:
            shards[mask] = exchange(kv_mine, ("seq", mask))
    queries = call(
        functools.partial(query_kernel, head=head, rows=block),
        "queries",
        (steps,),
        [smem_spec(), row_block(width), whole_spec(query_weight.shape), row_block(2), whole_spec(bounds.shape)],
        two_block,
        shape_of((2, token_count, LANES), LOW),
        flops=2 * token_count * width * width,
        moved=4 * token_count * width,
    )(place_of([0]), hidden, query_weight, routes, bounds)
    query_rows = queries.reshape(2 * token_count, LANES)
    row_count = 2 * token_count
    part = min(1024, row_count)
    parts = row_count // part

    def keys_of(masks):
        return jnp.concatenate([shards[m] for m in masks], axis=0) if len(masks) > 1 else shards[masks[0]]

    groups = [[0]] + mask_groups(seq_count, [1, 2, 3])
    state = None
    for index, masks in enumerate(groups):
        last = index == len(groups) - 1
        q_spec = pl.BlockSpec((part, LANES), lambda i, g: (i, 0))
        outs = (
            [shape_of((row_count, LANES), FULL), shape_of((row_count, LANES), LOW)]
            if last
            else shape_of((row_count, LANES), FULL)
        )
        state = call(
            functools.partial(forward_kernel, head=head, first=state is None, last=last),
            "attention_forward",
            (parts, len(masks)),
            [
                smem_spec(),
                q_spec,
                pl.BlockSpec((token_count, LANES), lambda i, g: (g, 0)),
                whole_spec(bounds.shape),
            ]
            + ([] if state is None else [q_spec]),
            [q_spec, q_spec] if last else q_spec,
            outs,
            [pltpu.VMEM((part, LANES), FULL)],
            flops=4 * row_count * token_count * len(masks) * 4 * head,
            moved=4 * row_count * LANES,
        )(place_of(masks), query_rows, keys_of(masks), bounds, *([] if state is None else [state]))
    attn, wide_queries = state

    out, grad_middle, grad_attn, grad_logits, grad_pair, grad_contract, grad_rows, grad_bias = call(
        functools.partial(middle_kernel, head=head),
        "feed_forward",
        (steps,),
        [
            row_block(width),
            row_block(width),
            two_block,
            row_block(LANES),
            row_block(2),
            whole_spec(vectors.shape),
            whole_spec(bias.shape),
            whole_spec(pair.shape),
            whole_spec(contract_all.shape),
        ],
        [
            row_block(width),
            row_block(width),
            two_block,
            row_block(LANES),
            whole_spec(pair.shape),
            whole_spec(contract_all.shape),
            whole_spec((8, width)),
            whole_spec((8, inner_width)),
        ],
        [
            shape_of((token_count, width), LOW),
            shape_of((token_count, width), FULL),
            shape_of((2, token_count, LANES), LOW),
            shape_of((token_count, LANES), LOW),
            shape_of(pair.shape, LOW),
            shape_of(contract_all.shape, LOW),
            shape_of((8, width), FULL),
            shape_of((8, inner_width), FULL),
        ],
        [pltpu.VMEM(pair.shape, FULL), pltpu.VMEM(contract_all.shape, FULL)],
        flops=2 * token_count * width * (3 * width + 6 * inner_width),
        moved=12 * width * inner_width,
    )(
        tokens, cotangent, attn.reshape(2, token_count, LANES), gates, routes, vectors, bias,
        pair, contract_all
    )

    grad_rows_in = grad_attn.reshape(row_count, LANES)
    grad_query = None
    kv_parts = {}
    for masks in mask_groups(seq_count, [2, 3, 1]) + [[0]]:
        q_spec = pl.BlockSpec((part, LANES), lambda g, i: (i, 0))
        k_spec = pl.BlockSpec((token_count, LANES), lambda g, i: (g, 0))
        full = whole_spec((row_count, LANES))
        grad_query, grad_keys = call(
            functools.partial(backward_kernel, head=head, first=grad_query is None, rows=part),
            "attention_backward",
            (len(masks), parts),
            [smem_spec(), q_spec, q_spec, k_spec, whole_spec(bounds.shape)]
            + ([] if grad_query is None else [full]),
            [full, k_spec],
            [
                shape_of((row_count, LANES), FULL),
                shape_of((token_count * len(masks), LANES), LOW),
            ],
            [pltpu.VMEM((token_count, LANES), FULL)],
            flops=10 * row_count * token_count * len(masks) * 4 * head,
            moved=8 * row_count * LANES,
        )(
            place_of(masks), wide_queries, grad_rows_in, keys_of(masks), bounds,
            *([] if grad_query is None else [grad_query])
        )
        for index, mask in enumerate(masks):
            piece = grad_keys[index * token_count : (index + 1) * token_count]
            kv_parts[mask] = piece if mask == 0 else exchange(piece, ("seq", mask))

    grad_hidden, grad_query_map, grad_router = call(
        functools.partial(placed_kernel, head=head),
        "query_gradient",
        (steps,),
        [
            two_block,
            row_block(width),
            row_block(2),
            row_block(LANES),
            whole_spec(query_weight.shape),
            whole_spec(side.shape),
        ],
        [row_block(width), whole_spec((width, width)), whole_spec((width, LANES))],
        [
            shape_of((token_count, width), FULL),
            shape_of((width, width), LOW),
            shape_of((width, LANES), FULL),
        ],
        [pltpu.VMEM((width, width), FULL), pltpu.VMEM((width, LANES), FULL)],
        flops=4 * token_count * width * width,
        moved=8 * token_count * width,
    )(grad_query.reshape(2, token_count, LANES), hidden, routes, grad_logits, query_weight, side)

    vector_rows = jnp.concatenate(
        [jnp.zeros((2, width), FULL), grad_rows[:3], grad_bias[0].reshape(width, extra).T[:3]]
    )
    spare = grad_bias[0].reshape(width, extra)[:, 3:]
    others = [kv_parts[m] for m in range(1, seq_count)]
    grad_tokens, grad_side = call(
        functools.partial(last_kernel, experts=experts, others=len(others)),
        "key_gradient",
        (steps,),
        [
            row_block(width),
            row_block(width),
            row_block(width),
            row_block(width),
            whole_spec(side.shape),
            whole_spec((8, width)),
            whole_spec((width, LANES)),
        ]
        + [row_block(LANES)] * (1 + len(others)),
        [row_block(width), whole_spec(side.shape)],
        [shape_of((token_count, width), LOW), shape_of(side.shape, LOW)],
        [pltpu.VMEM((width, LANES), FULL), pltpu.VMEM((8, width), FULL)],
        flops=4 * token_count * width * LANES,
        moved=12 * token_count * width,
    )(
        tokens, hidden, grad_hidden, grad_middle, side, vector_rows,
        grad_router + jnp.pad(spare, ((0, 0), (experts + 8, LANES - experts - 8 - spare.shape[1]))),
        kv_parts[0], *others
    )

    sum_pair = scatter_sum(grad_pair, order_a[::-1])
    sum_contract = scatter_sum(grad_contract[None], order_b[::-1])[0]
    sum_query = scatter_sum(grad_query_map[None], order_a[::-1])[0]
    sum_side = scatter_sum(grad_side[None], order_a[::-1])[0]
    sum_misc = sum_side[:, LANES:]
    sum_expand = jnp.concatenate([sum_pair[c + 1] for c in range(chunks)], axis=1)
    return (
        out,
        grad_tokens,
        sum_misc[:, experts],
        sum_misc[:, experts + 1],
        sum_misc[:, :experts],
        sum_query,
        sum_side[:, :LANES],
        sum_pair[0],
        sum_misc[:, experts + 2],
        sum_misc[:, experts + 3],
        sum_expand,
        sum_misc[:, experts + 5 : used].reshape(-1),
        sum_contract,
        sum_misc[:, experts + 4],
    )


def solution(mesh):
    both = ("dp", "seq")
    rows, vector = P(both, None), P(both)
    return jax.shard_map(
        per_device,
        mesh=mesh,
        in_specs=(
            rows, rows, P("dp", None), rows, vector, vector, rows, rows, rows, rows, vector, vector,
            rows, vector, rows, vector
        ),
        out_specs=(
            rows, rows, vector, vector, rows, rows, rows, rows, vector, vector, rows, vector, rows,
            vector
        ),
        check_vma=False,
    )
```

time: 1380 us -> 281 us (0.20)
  waiting for transfers between devices: 774 us -> 70.9 us
  blocking collectives: 357 us -> 0 us
  matrix products: 134 us -> 0 us
  Pallas kernels: 0 us -> 107 us
  starting transfers between devices: 0.41 us -> 39 us
  local copies, waits for them, and re-layouts: 52.5 us -> 32.1 us
    reduce_scatter x6 -> x0, waiting for transfers between devices: 665 us -> none  [the longest x1 149 us: per_device(): lax.psum_scatter(grad_expand, ('dp', 'seq'), scatter_dimension=0, tiled=T...]
    all_gather x4 -> x0, blocking collectives: 277 us -> none  [the longest x1 73.8 us: per_device(): lax.all_gather(to_low(output_map), ('dp', 'seq'), axis=0, tiled=True)]
    dot_general x73 -> x0, matrix products: 133 us -> none  [the longest x30 54.2 us: dot_last(): lax.dot_general(left_side, right_side, (((1,), (1,)), ((), ())), preferre...]
    unnamed x11 -> x0, waiting for transfers between devices: 109 us -> none
    pallas_call x0 -> x13, Pallas kernels: none -> 107 us  [the longest x4 38.1 us: per_device(): call(functools.partial(backward_kernel, head=head, first=grad_query is No...]
    unnamed x2 -> x0, blocking collectives: 79.4 us -> none
    ppermute x0 -> x41, waiting for transfers between devices: none -> 70.9 us  [exchange(): return lax.ppermute(block, axis, pairs)]
    ppermute x0 -> x41, starting transfers between devices: none -> 39 us  [exchange(): return lax.ppermute(block, axis, pairs)]
  transfers between devices with their start and end apart: 10 -> 41, of which waited for: 7 -> 22; matrix products, arithmetic and copies ran while one was open for 9% -> 15% of each run, Pallas kernels for 0% -> 27%
where the time goes in v1:
time: 281 us; the launch traced here: 277 us
  Pallas kernels  107 us (38%)
  waiting for transfers between devices  70.9 us (25%)
  starting transfers between devices  39 us (14%)
  local copies, waits for them, and re-layouts  32.1 us (11%)
  other arithmetic  26.5 us (9%)
    ppermute x41, waiting for transfers between devices, exchange(): return lax.ppermute(block, axis, pairs)  70.9 us
    ppermute x41, starting transfers between devices, exchange(): return lax.ppermute(block, axis, pairs)  39 us
    pallas_call x4, Pallas kernels, per_device(): call(functools.partial(backward_kernel, head=head, first=grad_query is No...  38.1 us
    pallas_call x1, Pallas kernels, per_device(): call(functools.partial(middle_kernel, head=head), 'feed_forward', (steps,...  30.6 us
    pallas_call x4, Pallas kernels, per_device(): call(functools.partial(forward_kernel, head=head, first=state is None, la...  23.4 us
    unnamed x60, local copies, waits for them, and re-layouts  9.51 us
    another operation x30, other arithmetic, gather_blocks(): block = jnp.stack([first, second], axis=position)  6.61 us
    dynamic_slice x2, local copies, waits for them, and re-layouts, scatter_sum(): keep = lax.dynamic_index_in_dim(value, bit, position, keepdims=False)  6.56 us
  transfers between devices with their start and end apart: 41, of which 22 were waited for; matrix products, arithmetic and copies ran while one was open for 15% of the time, Pallas kernels for 27%

profile of v1, /device:TPU:0, one launch (start us, length us, event | category | flops | bytes accessed | tf_op | source)
XLA Modules:
  0.0 277.3 jit_solution(3448409363406599939)
XLA Ops:
  1.6 3.1 %collective-permute-start.13 = (bf16[1,64,512]{2,1,0:T(8,128)(2,1)S(1)}, bf16[1,64,512]{2,1,0:T(8,128)(2,1)S(1)}, u32[]{:S(2)}, u32[]{:S(2)}) collective-permute-start(bf16[1,64,512]{2,1,0:T(8,128)(2,1)S(1)} %convert_bitcast_fusion), channel_id=1, source_target_pairs={{0,1},{1,0},{2,3},{3,2},{4,5},{5,4},{6,7},{7,6},{8,9},{9,8},{10,11... | collective-permute-start | bytes 196616 | tf_op jit(solution)/shard_map/ppermute | solution.py:51
  13.4 2.1 collective-permute-start
  18.1 2.7 collective-permute-start.1
  21.2 4.0 %collective-permute-done.1 = bf16[1,2,16,768]{3,2,1,0:T(8,128)(2,1)S(1)} collective-permute-done((bf16[1,2,16,768]{3,2,1,0:T(8,128)(2,1)S(1)}, bf16[1,2,16,768]{3,2,1,0:T(8,128)(2,1)S(1)}, u32[]{:S(2)}, u32[]{:S(2)}) %collective-permute-start.1) | collective-permute-done | bytes 49184 | tf_op jit(solution)/shard_map/ppermute | solution.py:51
  25.3 4.7 %collective-permute-start.2 = (bf16[1,2,2,16,768]{4,3,2,1,0:T(8,128)(2,1)S(1)}, bf16[1,2,2,16,768]{4,3,2,1,0:T(8,128)(2,1)S(1)}, u32[]{:S(2)}, u32[]{:S(2)}) collective-permute-start(bf16[1,2,2,16,768]{4,3,2,1,0:T(8,128)(2,1)S(1)} %pad_maximum_fusion.14), channel_id=1, source_target_pairs={{0,8},{4,12},{8,0},{12,4},{16,24},{20,28},{24,16},{28,20},{1,9},{5... | collective-permute-start | bytes 294920 | tf_op jit(solution)/shard_map/ppermute | solution.py:51
  30.1 2.5 collective-permute-done.2
  32.6 1.6 collective-permute-start.3
  34.9 2.9 %collective-permute-done.9 = bf16[5,2,16,512]{3,2,0,1:T(8,128)(2,1)S(1)} collective-permute-done((bf16[5,2,16,512]{3,2,0,1:T(8,128)(2,1)S(1)}, bf16[5,2,16,512]{3,2,0,1:T(8,128)(2,1)S(1)}, u32[]{:S(2)}, u32[]{:S(2)}) %collective-permute-start.9) | collective-permute-done | bytes 163872 | tf_op jit(solution)/shard_map/ppermute | solution.py:51
  38.7 2.6 collective-permute-done.15
  41.5 1.9 collective-permute-start.16
  43.4 4.5 %collective-permute-done.10 = bf16[5,2,2,16,512]{4,3,0,2,1:T(8,128)(2,1)S(1)} collective-permute-done((bf16[5,2,2,16,512]{4,3,0,2,1:T(8,128)(2,1)S(1)}, bf16[5,2,2,16,512]{4,3,0,2,1:T(8,128)(2,1)S(1)}, u32[]{:S(2)}, u32[]{:S(2)}) %collective-permute-start.10) | collective-permute-done | bytes 327712 | tf_op jit(solution)/shard_map/ppermute | solution.py:51
  48.0 1.6 collective-permute-start.11
  50.9 3.0 %hidden.1 = (bf16[1024,512]{1,0:T(8,128)(2,1)S(1)}, bf16[1024,128]{1,0:T(8,128)(2,1)}, f32[1024,128]{1,0:T(8,128)S(1)}) custom-call(bf16[1024,512]{1,0:T(8,128)(2,1)S(1)} %copy-done, bf16[512,256]{1,0:T(8,128)(2,1)S(1)} %slice.118.side_ref, s32[1024,2]{1,0:T(8,128)S(1)} %copy.60.routes_ref), custom_call_target="tpu_custom_call" | custom-call | flops 268435456 | bytes 2097152 | tf_op jit(solution)/shard_map/hidden/pallas_call | solution.py:557
  54.4 4.0 %collective-permute-start.5 = (bf16[1024,128]{1,0:T(8,128)(2,1)}, bf16[1024,128]{1,0:T(8,128)(2,1)}, u32[]{:S(2)}, u32[]{:S(2)}) collective-permute-start(bf16[1024,128]{1,0:T(8,128)(2,1)} %get-tuple-element.41.kv_ref), channel_id=1, source_target_pairs={{0,3},{1,2},{2,1},{3,0},{4,7},{5,6},{6,5},{7,4},{8,11},{9,10},{10,... | collective-permute-start | bytes 786440 | tf_op jit(solution)/shard_map/ppermute | solution.py:51
  62.6 2.2 queries.1
  64.8 5.5 %attention_forward.4.rest_0_ = f32[2048,128]{1,0:T(8,128)S(1)} custom-call(s32[1]{0:T(128)} %bitcast.1.place_ref, bf16[2048,128]{1,0:T(8,128)(2,1)S(1)} %bitcast.244, bf16[1024,128]{1,0:T(8,128)(2,1)} %get-tuple-element.41.kv_ref, s32[8,128]{1,0:T(8,128)S(1)} %pad.21.bounds_ref), custom_call_target="tpu_custom_call" | custom-call | flops 2147483648 | bytes 1048576 | tf_op jit(solution)/shard_map/attention_forward/pallas_call | solution.py:607
  76.6 5.2 %attention_forward.5.rest_0_ = f32[2048,128]{1,0:T(8,128)S(1)} custom-call(s32[1]{0:T(128)} %bitcast.28.place_ref, bf16[2048,128]{1,0:T(8,128)(2,1)S(1)} %bitcast.245, bf16[1024,128]{1,0:T(8,128)(2,1)} %collective-permute-done.7.kv_ref, s32[8,128]{1,0:T(8,128)S(1)} %pad.21.bounds_ref, f32[2048,128]{1,0:T(8,128)S(1)} %copy-done.13), custom_call_target="tpu_custom_call" | custom-call | flops 2147483648 | bytes 1048576 | tf_op jit(solution)/shard_map/attention_forward/pallas_call | solution.py:607
  81.9 5.3 %attention_forward.6.rest_0_ = f32[2048,128]{1,0:T(8,128)S(1)} custom-call(s32[1]{0:T(128)} %bitcast.27.place_ref, bf16[2048,128]{1,0:T(8,128)(2,1)S(1)} %bitcast.246, bf16[1024,128]{1,0:T(8,128)(2,1)} %collective-permute-done.6.kv_ref, s32[8,128]{1,0:T(8,128)S(1)} %pad.21.bounds_ref, f32[2048,128]{1,0:T(8,128)S(1)} %attention_forward.5.rest_0_), custom_call_target="tpu_custom_call" | custom-call | flops 2147483648 | bytes 1048576 | tf_op jit(solution)/shard_map/attention_forward/pallas_call | solution.py:607
  87.2 7.4 %attention_forward.7 = (f32[2048,128]{1,0:T(8,128)S(1)}, bf16[2048,128]{1,0:T(8,128)(2,1)S(1)}) custom-call(s32[1]{0:T(128)} %bitcast.place_ref, bf16[2048,128]{1,0:T(8,128)(2,1)S(1)} %bitcast.247, bf16[1024,128]{1,0:T(8,128)(2,1)} %collective-permute-done.5.kv_ref, s32[8,128]{1,0:T(8,128)S(1)} %pad.21.bounds_ref, f32[2048,128]{1,0:T(8,128)S(1)} %attention_forward.6.rest_0_), custom_call_target="tpu_custom_call" | custom-call | flops 2147483648 | bytes 1048576 | tf_op jit(solution)/shard_map/attention_forward/pallas_call | solution.py:607
  96.2 1.6 copy.63
  99.6 1.8 copy.62
  101.4 30.6 %feed_forward.1 = (bf16[1024,512]{1,0:T(8,128)(2,1)}, f32[1024,512]{1,0:T(8,128)}, bf16[2,1024,128]{2,1,0:T(8,128)(2,1)S(1)}, bf16[1024,128]{1,0:T(8,128)(2,1)S(...) custom-call(bf16[1024,512]{1,0:T(8,128)(2,1)S(1)} %copy-done, ...), custom_call_target="tpu_custom_call" | custom-call | flops 14495514624 | bytes 12582912 | tf_op jit(solution)/shard_map/feed_forward/pallas_call | solution.py:626
  132.1 2.8 %constant_dynamic-slice_fusion.1 = (bf16[1,2,2,1,2,2,64,512]{7,6,5,4,3,2,1,0:T(8,128)(2,1)}, bf16[1,2,2,1,2,2,64,512]{7,6,5,4,3,2,1,0:T(8,128)(2,1)S(1)}) fusion(bf16[1,2,2,2,2,2,64,512]{7,6,5,4,3,2,1,0:T(8,128)(2,1)} %bitcast.261, s32[]{:T(128)S(6)} %select_n.351, s32[]{:T(128)S(6)} %select_n.352), kind=kLoop, calls=%fused_computation.127 | loop fusion | bytes 4194312 | tf_op jit(solution)/shard_map/jit(dynamic_index_in_dim)/dynamic_slice | solution.py:87
  136.0 9.4 %attention_backward.4 = (f32[2048,128]{1,0:T(8,128)S(1)}, bf16[1024,128]{1,0:T(8,128)(2,1)}) custom-call(s32[1]{0:T(128)} %bitcast.27.place_ref, bf16[2048,128]{1,0:T(8,128)(2,1)S(1)} %get-tuple-element.45.query_ref, bf16[2048,128]{1,0:T(8,128)(2,1)S(1)} %bitcast.252, bf16[1024,128]{1,0:T(8,128)(2,1)} %collective-permute-done.6.kv_ref, ...), custom_call_target="tpu_custom_call" | custom-call | flops 5368709120 | bytes 2097152 | tf_op jit(solution)/shard_map/attention_backward/pallas_call | solution.py:676
  145.4 9.9 %attention_backward.5 = (f32[2048,128]{1,0:T(8,128)S(1)}, bf16[1024,128]{1,0:T(8,128)(2,1)}) custom-call(s32[1]{0:T(128)} %bitcast.place_ref, bf16[2048,128]{1,0:T(8,128)(2,1)S(1)} %get-tuple-element.45.query_ref, bf16[2048,128]{1,0:T(8,128)(2,1)S(1)} %bitcast.253, bf16[1024,128]{1,0:T(8,128)(2,1)} %collective-permute-done.5.kv_ref, ...), custom_call_target="tpu_custom_call" | custom-call | flops 5368709120 | bytes 2097152 | tf_op jit(solution)/shard_map/attention_backward/pallas_call | solution.py:676
  155.2 9.5 %attention_backward.6 = (f32[2048,128]{1,0:T(8,128)S(1)}, bf16[1024,128]{1,0:T(8,128)(2,1)}) custom-call(s32[1]{0:T(128)} %bitcast.28.place_ref, bf16[2048,128]{1,0:T(8,128)(2,1)S(1)} %get-tuple-element.45.query_ref, bf16[2048,128]{1,0:T(8,128)(2,1)S(1)} %bitcast.254, bf16[1024,128]{1,0:T(8,128)(2,1)} %collective-permute-done.7.kv_ref, ...), custom_call_target="tpu_custom_call" | custom-call | flops 5368709120 | bytes 2097152 | tf_op jit(solution)/shard_map/attention_backward/pallas_call | solution.py:676
  164.7 9.4 %attention_backward.7 = (f32[2048,128]{1,0:T(8,128)S(1)}, bf16[1024,128]{1,0:T(8,128)(2,1)S(1)}) custom-call(s32[1]{0:T(128)} %bitcast.1.place_ref, bf16[2048,128]{1,0:T(8,128)(2,1)S(1)} %get-tuple-element.45.query_ref, bf16[2048,128]{1,0:T(8,128)(2,1)S(1)} %bitcast.255, bf16[1024,128]{1,0:T(8,128)(2,1)} %get-tuple-element.41.kv_ref, ...), custom_call_target="tpu_custom_call" | custom-call | flops 5368709120 | bytes 2097152 | tf_op jit(solution)/shard_map/attention_backward/pallas_call | solution.py:676
  174.9 4.6 %query_gradient.1 = (f32[1024,512]{1,0:T(8,128)}, bf16[512,512]{1,0:T(8,128)(2,1)S(1)}, f32[512,128]{1,0:T(8,128)S(1)}) custom-call(f32[2,1024,128]{2,1,0:T(8,128)S(1)} %bitcast.251, bf16[1024,512]{1,0:T(8,128)(2,1)S(1)} %get-tuple-element.40.hidden_ref, s32[1024,2]{1,0:T(8,128)S(1)} %copy.60.routes_ref, ...), custom_call_target="tpu_custom_call" | custom-call | flops 1073741824 | bytes 4194304 | tf_op jit(solution)/shard_map/query_gradient/pallas_call | solution.py:698
  183.0 2.9 %collective-permute-start.19 = (bf16[1024,128]{1,0:T(8,128)(2,1)}, bf16[1024,128]{1,0:T(8,128)(2,1)S(1)}, u32[]{:S(2)}, u32[]{:S(2)}) collective-permute-start(bf16[1024,128]{1,0:T(8,128)(2,1)} %get-tuple-element.59), channel_id=1, source_target_pairs={{0,2},{1,3},{2,0},{3,1},{4,6},{5,7},{6,4},{7,5},{8,10},{9,11},{10,... | collective-permute-start | bytes 786440 | tf_op jit(solution)/shard_map/ppermute | solution.py:51
  187.0 3.7 %constant_dynamic-slice_fusion.3 = (bf16[5,2,2,1,2,2,16,512]{7,6,5,4,3,2,1,0:T(8,128)(2,1)}, bf16[5,2,2,1,2,2,16,512]{7,6,5,4,3,2,1,0:T(8,128)(2,1)}) fusion(bf16[5,2,2,2,2,2,16,512]{7,6,5,4,3,2,1,0:T(8,128)(2,1)} %bitcast.260, s32[]{:T(128)S(6)} %select_n.351, s32[]{:T(128)S(6)} %select_n.352), kind=kLoop, calls=%fused_computation.129 | loop fusion | bytes 5242888 | tf_op jit(solution)/shard_map/jit(dynamic_index_in_dim)/dynamic_slice | solution.py:87
  191.8 1.6 copy.88
  193.5 3.0 %collective-permute-done.18.rest_0_ = bf16[1024,128]{1,0:T(8,128)(2,1)S(1)} collective-permute-done((bf16[1024,128]{1,0:T(8,128)(2,1)}, bf16[1024,128]{1,0:T(8,128)(2,1)S(1)}, u32[]{:S(2)}, u32[]{:S(2)}) %collective-permute-start.18) | collective-permute-done | bytes 262176 | tf_op jit(solution)/shard_map/ppermute | solution.py:51
  196.5 12.4 %collective-permute-done.19.rest_1_ = bf16[1024,128]{1,0:T(8,128)(2,1)S(1)} collective-permute-done((bf16[1024,128]{1,0:T(8,128)(2,1)}, bf16[1024,128]{1,0:T(8,128)(2,1)S(1)}, u32[]{:S(2)}, u32[]{:S(2)}) %collective-permute-start.19) | collective-permute-done | bytes 262176 | tf_op jit(solution)/shard_map/ppermute | solution.py:51
  209.0 4.9 %key_gradient.1 = (bf16[1024,512]{1,0:T(8,128)(2,1)}, bf16[512,256]{1,0:T(8,128)(2,1)S(1)}) custom-call(bf16[1024,512]{1,0:T(8,128)(2,1)S(1)} %copy-done, bf16[1024,512]{1,0:T(8,128)(2,1)S(1)} %get-tuple-element.40.hidden_ref, f32[1024,512]{1,0:T(8,128)S(1)} %copy-done.1, f32[1024,512]{1,0:T(8,128)} %get-tuple-element.53.grad_middle_ref, ...), custom_call_target="tpu_custom_call" | custom-call | flops 268435456 | bytes 6291456 | tf_op jit(solution)/shard_map/key_gradient/pallas_call | solution.py:726
  215.7 1.6 collective-permute-start.22
  217.3 4.1 %collective-permute-done.27 = bf16[1,2,2,2,16,512]{5,4,3,2,1,0:T(8,128)(2,1)S(1)} collective-permute-done((bf16[1,2,2,2,16,512]{5,4,3,2,1,0:T(8,128)(2,1)S(1)}, bf16[1,2,2,2,16,512]{5,4,3,2,1,0:T(8,128)(2,1)S(1)}, u32[]{:S(2)}, u32[]{:S(2)}) %collective-permute-start.27) | collective-permute-done | bytes 131104 | tf_op jit(solution)/shard_map/ppermute | solution.py:51
  223.7 2.2 collective-permute-done.28
  226.5 2.5 collective-permute-start.24
  229.0 1.9 collective-permute-done.29
  231.2 1.9 collective-permute-start.25
  233.1 1.6 collective-permute-done.30
  235.4 1.6 convert_add_fusion.1
  242.5 6.0 %collective-permute-done.37 = bf16[1,2,2,2,64,512]{5,4,3,2,1,0:T(8,128)(2,1)} collective-permute-done((bf16[1,2,2,2,64,512]{5,4,3,2,1,0:T(8,128)(2,1)}, bf16[1,2,2,2,64,512]{5,4,3,2,1,0:T(8,128)(2,1)}, u32[]{:S(2)}, u32[]{:S(2)}) %collective-permute-start.37) | collective-permute-done | bytes 524320 | tf_op jit(solution)/shard_map/ppermute | solution.py:51
  250.7 4.4 %collective-permute-done.32 = bf16[5,2,2,2,16,512]{5,4,0,3,2,1:T(8,128)(2,1)} collective-permute-done((bf16[5,2,2,2,16,512]{5,4,0,3,2,1:T(8,128)(2,1)S(1)}, bf16[5,2,2,2,16,512]{5,4,0,3,2,1:T(8,128)(2,1)}, u32[]{:S(2)}, u32[]{:S(2)}) %collective-permute-start.32) | collective-permute-done | bytes 655392 | tf_op jit(solution)/shard_map/ppermute | solution.py:51
  258.0 5.6 %collective-permute-done.33 = bf16[5,2,2,16,512]{4,3,0,2,1:T(8,128)(2,1)S(1)} collective-permute-done((bf16[5,2,2,16,512]{4,3,0,2,1:T(8,128)(2,1)S(1)}, bf16[5,2,2,16,512]{4,3,0,2,1:T(8,128)(2,1)S(1)}, u32[]{:S(2)}, u32[]{:S(2)}) %collective-permute-start.33) | collective-permute-done | bytes 327712 | tf_op jit(solution)/shard_map/ppermute | solution.py:51
  263.8 2.2 collective-permute-done.39
  266.2 5.0 %collective-permute-done.34 = bf16[5,2,16,512]{3,2,0,1:T(8,128)(2,1)S(1)} collective-permute-done((bf16[5,2,16,512]{3,2,0,1:T(8,128)(2,1)S(1)}, bf16[5,2,16,512]{3,2,0,1:T(8,128)(2,1)S(1)}, u32[]{:S(2)}, u32[]{:S(2)}) %collective-permute-start.34) | collective-permute-done | bytes 163872 | tf_op jit(solution)/shard_map/ppermute | solution.py:51
  272.7 3.1 %collective-permute-done.35 = bf16[5,16,512]{2,1,0:T(8,128)(2,1)S(1)} collective-permute-done((bf16[5,16,512]{2,1,0:T(8,128)(2,1)S(1)}, bf16[5,16,512]{2,1,0:T(8,128)(2,1)S(1)}, u32[]{:S(2)}, u32[]{:S(2)}) %collective-permute-start.35) | collective-permute-done | bytes 81952 | tf_op jit(solution)/shard_map/ppermute | solution.py:51
  (232 shorter events, 56.7 us)
Async XLA Ops:
  0.6 20.1 %copy-start.26 = (f32[64,512]{1,0:T(8,128)S(1)}, f32[64,512]{1,0:T(8,128)}, u32[]{:S(2)}) copy-start(f32[64,512]{1,0:T(8,128)} %param.30) | copy-start | bytes 393220
  1.6 19.1 %collective-permute-start.13 = (bf16[1,64,512]{2,1,0:T(8,128)(2,1)S(1)}, bf16[1,64,512]{2,1,0:T(8,128)(2,1)S(1)}, u32[]{:S(2)}, u32[]{:S(2)}) collective-permute-start(bf16[1,64,512]{2,1,0:T(8,128)(2,1)S(1)} %convert_bitcast_fusion), channel_id=1, source_target_pairs={{0,1},{1,0},{2,3},{3,2},{4,5},{5,4},{6,7},{7,6},{8,9},{9,8},{10,11... | collective-permute-start | bytes 196616 | tf_op jit(solution)/shard_map/ppermute | solution.py:51
  6.4 23.6 %collective-permute-start.8 = (bf16[5,16,512]{2,1,0:T(8,128)(2,1)S(1)}, bf16[5,16,512]{2,1,0:T(8,128)(2,1)S(1)}, u32[]{:S(2)}, u32[]{:S(2)}) collective-permute-start(bf16[5,16,512]{2,1,0:T(8,128)(2,1)S(1)} %fusion.17), channel_id=1, source_target_pairs={{0,1},{1,0},{2,3},{3,2},{4,5},{5,4},{6,7},{7,6},{8,9},{9,8},{10,11... | collective-permute-start | bytes 245768 | tf_op jit(solution)/shard_map/ppermute | solution.py:51
  13.4 4.7 %collective-permute-start = (bf16[1,16,768]{2,1,0:T(8,128)(2,1)S(1)}, bf16[1,16,768]{2,1,0:T(8,128)(2,1)S(1)}, u32[]{:S(2)}, u32[]{:S(2)}) collective-permute-start(bf16[1,16,768]{2,1,0:T(8,128)(2,1)S(1)} %concatenate.44), channel_id=1, source_target_pairs={{0,1},{1,0},{2,3},{3,2},{4,5},{5,4},{6,7},{7,6},{8,9},{9,8},{10,11... | collective-permute-start | bytes 73736 | tf_op jit(solution)/shard_map/ppermute | solution.py:51
  18.1 7.2 %collective-permute-start.1 = (bf16[1,2,16,768]{3,2,1,0:T(8,128)(2,1)S(1)}, bf16[1,2,16,768]{3,2,1,0:T(8,128)(2,1)S(1)}, u32[]{:S(2)}, u32[]{:S(2)}) collective-permute-start(bf16[1,2,16,768]{3,2,1,0:T(8,128)(2,1)S(1)} %pad_maximum_fusion.15), channel_id=1, source_target_pairs={{0,2},{1,3},{2,0},{3,1},{4,6},{5,7},{6,4},{7,5},{8,10},{9,11},{10,... | collective-permute-start | bytes 147464 | tf_op jit(solution)/shard_map/ppermute | solution.py:51
  20.8 13.4 %collective-permute-start.14 = (bf16[1,2,64,512]{3,2,1,0:T(8,128)(2,1)S(1)}, bf16[1,2,64,512]{3,2,1,0:T(8,128)(2,1)S(1)}, u32[]{:S(2)}, u32[]{:S(2)}) collective-permute-start(bf16[1,2,64,512]{3,2,1,0:T(8,128)(2,1)S(1)} %pad_maximum_fusion.12), channel_id=1, source_target_pairs={{0,2},{1,3},{2,0},{3,1},{4,6},{5,7},{6,4},{7,5},{8,10},{9,11},{10,... | collective-permute-start | bytes 393224 | tf_op jit(solution)/shard_map/ppermute | solution.py:51
  25.3 7.3 %collective-permute-start.2 = (bf16[1,2,2,16,768]{4,3,2,1,0:T(8,128)(2,1)S(1)}, bf16[1,2,2,16,768]{4,3,2,1,0:T(8,128)(2,1)S(1)}, u32[]{:S(2)}, u32[]{:S(2)}) collective-permute-start(bf16[1,2,2,16,768]{4,3,2,1,0:T(8,128)(2,1)S(1)} %pad_maximum_fusion.14), channel_id=1, source_target_pairs={{0,8},{4,12},{8,0},{12,4},{16,24},{20,28},{24,16},{28,20},{1,9},{5... | collective-permute-start | bytes 294920 | tf_op jit(solution)/shard_map/ppermute | solution.py:51
  30.0 7.7 %collective-permute-start.9 = (bf16[5,2,16,512]{3,2,0,1:T(8,128)(2,1)S(1)}, bf16[5,2,16,512]{3,2,0,1:T(8,128)(2,1)S(1)}, u32[]{:S(2)}, u32[]{:S(2)}) collective-permute-start(bf16[5,2,16,512]{3,2,0,1:T(8,128)(2,1)S(1)} %pad_maximum_fusion.11), channel_id=1, source_target_pairs={{0,2},{1,3},{2,0},{3,1},{4,6},{5,7},{6,4},{7,5},{8,10},{9,11},{10,... | collective-permute-start | bytes 491528 | tf_op jit(solution)/shard_map/ppermute | solution.py:51
  32.6 5.9 %collective-permute-start.3 = (bf16[1,2,2,2,16,768]{5,4,3,2,1,0:T(8,128)(2,1)S(1)}, bf16[1,2,2,2,16,768]{5,4,3,2,1,0:T(8,128)(2,1)S(1)}, u32[]{:S(2)}, u32[]{:S(2)}) collective-permute-start(bf16[1,2,2,2,16,768]{5,4,3,2,1,0:T(8,128)(2,1)S(1)} %pad_maximum_fusion.10), channel_id=1, source_target_pairs={{0,16},{4,20},{8,24},{12,28},{16,0},{20,4},{24,8},{28,12},{1,17},{... | collective-permute-start | bytes 589832 | tf_op jit(solution)/shard_map/ppermute | solution.py:51
  34.3 7.1 %collective-permute-start.15 = (bf16[1,2,2,64,512]{4,3,2,1,0:T(8,128)(2,1)S(1)}, bf16[1,2,2,64,512]{4,3,2,1,0:T(8,128)(2,1)S(1)}, u32[]{:S(2)}, u32[]{:S(2)}) collective-permute-start(bf16[1,2,2,64,512]{4,3,2,1,0:T(8,128)(2,1)S(1)} %pad_maximum_fusion.9), channel_id=1, source_target_pairs={{0,16},{4,20},{8,24},{12,28},{16,0},{20,4},{24,8},{28,12},{1,17},{... | collective-permute-start | bytes 786440 | tf_op jit(solution)/shard_map/ppermute | solution.py:51
  37.8 10.0 %collective-permute-start.10 = (bf16[5,2,2,16,512]{4,3,0,2,1:T(8,128)(2,1)S(1)}, bf16[5,2,2,16,512]{4,3,0,2,1:T(8,128)(2,1)S(1)}, u32[]{:S(2)}, u32[]{:S(2)}) collective-permute-start(bf16[5,2,2,16,512]{4,3,0,2,1:T(8,128)(2,1)S(1)} %pad_maximum_fusion.8), channel_id=1, source_target_pairs={{0,8},{4,12},{8,0},{12,4},{16,24},{20,28},{24,16},{28,20},{1,9},{5... | collective-permute-start | bytes 983048 | tf_op jit(solution)/shard_map/ppermute | solution.py:51
  38.6 10.9 %collective-permute-start.4 = (bf16[1,2,2,2,2,16,768]{6,5,4,3,2,1,0:T(8,128)(2,1)S(1)}, bf16[1,2,2,2,2,16,768]{6,5,4,3,2,1,0:T(8,128)(2,1)S(1)}, u32[]{:S(2)}, u32[]{:S(2)}) collective-permute-start(bf16[1,2,2,2,2,16,768]{6,5,4,3,2,1,0:T(8,128)(2,1)S(1)} %pad_maximum_fusion.7), channel_id=1, source_target_pairs={{0,4},{4,0},{8,12},{12,8},{16,20},{20,16},{24,28},{28,24},{1,5},{5... | collective-permute-start | bytes 1179656 | tf_op jit(solution)/shard_map/ppermute | solution.py:51
  41.5 17.7 %collective-permute-start.16 = (bf16[1,2,2,2,64,512]{5,4,3,2,1,0:T(8,128)(2,1)S(1)}, bf16[1,2,2,2,64,512]{5,4,3,2,1,0:T(8,128)(2,1)S(1)}, u32[]{:S(2)}, u32[]{:S(2)}) collective-permute-start(bf16[1,2,2,2,64,512]{5,4,3,2,1,0:T(8,128)(2,1)S(1)} %pad_maximum_fusion.6), channel_id=1, source_target_pairs={{0,8},{4,12},{8,0},{12,4},{16,24},{20,28},{24,16},{28,20},{1,9},{5... | collective-permute-start | bytes 1572872 | tf_op jit(solution)/shard_map/ppermute | solution.py:51
  48.0 12.5 %collective-permute-start.11 = (bf16[5,2,2,2,16,512]{5,4,0,3,2,1:T(8,128)(2,1)S(1)}, bf16[5,2,2,2,16,512]{5,4,0,3,2,1:T(8,128)(2,1)S(1)}, u32[]{:S(2)}, u32[]{:S(2)}) collective-permute-start(bf16[5,2,2,2,16,512]{5,4,0,3,2,1:T(8,128)(2,1)S(1)} %pad_maximum_fusion.5), channel_id=1, source_target_pairs={{0,16},{4,20},{8,24},{12,28},{16,0},{20,4},{24,8},{28,12},{1,17},{... | collective-permute-start | bytes 1966088 | tf_op jit(solution)/shard_map/ppermute | solution.py:51
  54.0 20.4 %collective-permute-start.7 = (bf16[1024,128]{1,0:T(8,128)(2,1)}, bf16[1024,128]{1,0:T(8,128)(2,1)}, u32[]{:S(2)}, u32[]{:S(2)}) collective-permute-start(bf16[1024,128]{1,0:T(8,128)(2,1)} %get-tuple-element.41.kv_ref), channel_id=1, source_target_pairs={{0,1},{1,0},{2,3},{3,2},{4,5},{5,4},{6,7},{7,6},{8,9},{9,8},{10,11... | collective-permute-start | bytes 786440 | tf_op jit(solution)/shard_map/ppermute | solution.py:51
  54.0 27.9 %collective-permute-start.6 = (bf16[1024,128]{1,0:T(8,128)(2,1)}, bf16[1024,128]{1,0:T(8,128)(2,1)}, u32[]{:S(2)}, u32[]{:S(2)}) collective-permute-start(bf16[1024,128]{1,0:T(8,128)(2,1)} %get-tuple-element.41.kv_ref), channel_id=1, source_target_pairs={{0,2},{1,3},{2,0},{3,1},{4,6},{5,7},{6,4},{7,5},{8,10},{9,11},{10,... | collective-permute-start | bytes 786440 | tf_op jit(solution)/shard_map/ppermute | solution.py:51
  54.4 32.8 %collective-permute-start.5 = (bf16[1024,128]{1,0:T(8,128)(2,1)}, bf16[1024,128]{1,0:T(8,128)(2,1)}, u32[]{:S(2)}, u32[]{:S(2)}) collective-permute-start(bf16[1024,128]{1,0:T(8,128)(2,1)} %get-tuple-element.41.kv_ref), channel_id=1, source_target_pairs={{0,3},{1,2},{2,1},{3,0},{4,7},{5,6},{6,5},{7,4},{8,11},{9,10},{10,... | collective-permute-start | bytes 786440 | tf_op jit(solution)/shard_map/ppermute | solution.py:51
  60.4 34.2 %collective-permute-start.17 = (bf16[1,2,2,2,2,64,512]{6,5,4,3,1,2,0:T(8,128)(2,1)}, bf16[1,2,2,2,2,64,512]{6,5,4,3,1,2,0:T(8,128)(2,1)}, u32[]{:S(2)}, u32[]{:S(2)}) collective-permute-start(bf16[1,2,2,2,2,64,512]{6,5,4,3,1,2,0:T(8,128)(2,1)} %pad_maximum_fusion.3), channel_id=1, source_target_pairs={{0,4},{4,0},{8,12},{12,8},{16,20},{20,16},{24,28},{28,24},{1,5},{5... | collective-permute-start | bytes 3145736 | tf_op jit(solution)/shard_map/ppermute | solution.py:51
  62.1 35.7 %collective-permute-start.12 = (bf16[5,2,2,2,2,16,512]{6,5,0,4,3,2,1:T(8,128)(2,1)}, bf16[5,2,2,2,2,16,512]{6,5,0,4,3,2,1:T(8,128)(2,1)}, u32[]{:S(2)}, u32[]{:S(2)}) collective-permute-start(bf16[5,2,2,2,2,16,512]{6,5,0,4,3,2,1:T(8,128)(2,1)} %pad_maximum_fusion.2), channel_id=1, source_target_pairs={{0,4},{4,0},{8,12},{12,8},{16,20},{20,16},{24,28},{28,24},{1,5},{5... | collective-permute-start | bytes 3932168 | tf_op jit(solution)/shard_map/ppermute | solution.py:51
  64.8 5.5 %copy-start.4 = (bf16[2,1024,128]{2,1,0:T(8,128)(2,1)}, bf16[2,1024,128]{2,1,0:T(8,128)(2,1)S(1)}, u32[]{:S(2)}) copy-start(bf16[2,1024,128]{2,1,0:T(8,128)(2,1)S(1)} %queries.1) | copy-start | bytes 1572868
  87.2 7.4 %copy-start.21 = (bf16[1,2,1,2,2,64,512]{6,5,4,3,1,2,0:T(8,128)(2,1)S(1)}, bf16[1,2,1,2,2,64,512]{6,5,4,3,1,2,0:T(8,128)(2,1)}, u32[]{:S(2)}) copy-start(bf16[1,2,1,2,2,64,512]{6,5,4,3,1,2,0:T(8,128)(2,1)} %copy-done.20) | copy-start | bytes 1572868
  87.2 7.4 %copy-start.23 = (bf16[1,2,1,2,2,64,512]{6,5,4,3,1,2,0:T(8,128)(2,1)S(1)}, bf16[1,2,1,2,2,64,512]{6,5,4,3,1,2,0:T(8,128)(2,1)}, u32[]{:S(2)}) copy-start(bf16[1,2,1,2,2,64,512]{6,5,4,3,1,2,0:T(8,128)(2,1)} %copy-done.22) | copy-start | bytes 1572868
  136.0 99.4 %collective-permute-start.36 = (bf16[1,2,2,2,2,64,512]{6,5,4,3,1,2,0:T(8,128)(2,1)}, bf16[1,2,2,2,2,64,512]{6,5,4,3,1,2,0:T(8,128)(2,1)}, u32[]{:S(2)}, u32[]{:S(2)}) collective-permute-start(bf16[1,2,2,2,2,64,512]{6,5,4,3,1,2,0:T(8,128)(2,1)} %bitcast.240), channel_id=1, source_target_pairs={{0,4},{4,0},{8,12},{12,8},{16,20},{20,16},{24,28},{28,24},{1,5},{5... | collective-permute-start | bytes 3145736 | tf_op jit(solution)/shard_map/ppermute | solution.py:51
  181.0 33.0 %collective-permute-start.26 = (bf16[1,2,2,2,2,16,512]{6,5,4,3,2,1,0:T(8,128)(2,1)}, bf16[1,2,2,2,2,16,512]{6,5,4,3,2,1,0:T(8,128)(2,1)}, u32[]{:S(2)}, u32[]{:S(2)}) collective-permute-start(bf16[1,2,2,2,2,16,512]{6,5,4,3,2,1,0:T(8,128)(2,1)} %dynamic-slice_bitcast_fusion), channel_id=1, source_target_pairs={{0,4},{4,0},{8,12},{12,8},{16,20},{20,16},{24,28},{28,24},{1,5},{5... | collective-permute-start | bytes 786440 | tf_op jit(solution)/shard_map/ppermute | solution.py:51
  182.5 14.1 %collective-permute-start.18 = (bf16[1024,128]{1,0:T(8,128)(2,1)}, bf16[1024,128]{1,0:T(8,128)(2,1)S(1)}, u32[]{:S(2)}, u32[]{:S(2)}) collective-permute-start(bf16[1024,128]{1,0:T(8,128)(2,1)} %get-tuple-element.58), channel_id=1, source_target_pairs={{0,1},{1,0},{2,3},{3,2},{4,5},{5,4},{6,7},{7,6},{8,9},{9,8},{10,11... | collective-permute-start | bytes 786440 | tf_op jit(solution)/shard_map/ppermute | solution.py:51
  182.5 14.1 %collective-permute-start.20 = (bf16[1024,128]{1,0:T(8,128)(2,1)}, bf16[1024,128]{1,0:T(8,128)(2,1)S(1)}, u32[]{:S(2)}, u32[]{:S(2)}) collective-permute-start(bf16[1024,128]{1,0:T(8,128)(2,1)} %get-tuple-element.60), channel_id=1, source_target_pairs={{0,3},{1,2},{2,1},{3,0},{4,7},{5,6},{6,5},{7,4},{8,11},{9,10},{10,... | collective-permute-start | bytes 786440 | tf_op jit(solution)/shard_map/ppermute | solution.py:51
  183.0 25.9 %collective-permute-start.19 = (bf16[1024,128]{1,0:T(8,128)(2,1)}, bf16[1024,128]{1,0:T(8,128)(2,1)S(1)}, u32[]{:S(2)}, u32[]{:S(2)}) collective-permute-start(bf16[1024,128]{1,0:T(8,128)(2,1)} %get-tuple-element.59), channel_id=1, source_target_pairs={{0,2},{1,3},{2,0},{3,1},{4,6},{5,7},{6,4},{7,5},{8,10},{9,11},{10,... | collective-permute-start | bytes 786440 | tf_op jit(solution)/shard_map/ppermute | solution.py:51
  191.8 17.1 %copy-start.1 = (f32[1024,512]{1,0:T(8,128)S(1)}, f32[1024,512]{1,0:T(8,128)}, u32[]{:S(2)}) copy-start(f32[1024,512]{1,0:T(8,128)} %get-tuple-element.52.grad_hidden_ref) | copy-start | bytes 6291460
  191.8 17.1 %copy-start.7 = (bf16[1024,128]{1,0:T(8,128)(2,1)S(1)}, bf16[1024,128]{1,0:T(8,128)(2,1)}, u32[]{:S(2)}) copy-start(bf16[1024,128]{1,0:T(8,128)(2,1)} %copy-done.6) | copy-start | bytes 786436
  196.5 41.8 %collective-permute-start.31 = (bf16[5,2,2,2,2,16,512]{6,5,0,4,3,2,1:T(8,128)(2,1)S(1)}, bf16[5,2,2,2,2,16,512]{6,5,0,4,3,2,1:T(8,128)(2,1)S(1)}, u32[]{:S(2)}, u32[]{:S(2)}) collective-permute-start(bf16[5,2,2,2,2,16,512]{6,5,0,4,3,2,1:T(8,128)(2,1)S(1)} %bitcast.263), channel_id=1, source_target_pairs={{0,4},{4,0},{8,12},{12,8},{16,20},{20,16},{24,28},{28,24},{1,5},{5... | collective-permute-start | bytes 3932168 | tf_op jit(solution)/shard_map/ppermute | solution.py:51
  213.9 1.8 collective-permute-start.21
  215.0 20.3 %copy-start.24 = (bf16[1,2,2,1,2,2,64,512]{7,6,5,4,3,2,1,0:T(8,128)(2,1)S(1)}, bf16[1,2,2,1,2,2,64,512]{7,6,5,4,3,2,1,0:T(8,128)(2,1)}, u32[]{:S(2)}) copy-start(bf16[1,2,2,1,2,2,64,512]{7,6,5,4,3,2,1,0:T(8,128)(2,1)} %get-tuple-element.103) | copy-start | bytes 3145732
  215.1 6.4 %collective-permute-start.27 = (bf16[1,2,2,2,16,512]{5,4,3,2,1,0:T(8,128)(2,1)S(1)}, bf16[1,2,2,2,16,512]{5,4,3,2,1,0:T(8,128)(2,1)S(1)}, u32[]{:S(2)}, u32[]{:S(2)}) collective-permute-start(bf16[1,2,2,2,16,512]{5,4,3,2,1,0:T(8,128)(2,1)S(1)} %fusion.5), channel_id=1, source_target_pairs={{0,16},{4,20},{8,24},{12,28},{16,0},{20,4},{24,8},{28,12},{1,17},{... | collective-permute-start | bytes 393224 | tf_op jit(solution)/shard_map/ppermute | solution.py:51
  215.7 6.7 %collective-permute-start.22 = (bf16[1,2,2,2,16,256]{5,4,3,2,1,0:T(8,128)(2,1)S(1)}, bf16[1,2,2,2,16,256]{5,4,3,2,1,0:T(8,128)(2,1)S(1)}, u32[]{:S(2)}, u32[]{:S(2)}) collective-permute-start(bf16[1,2,2,2,16,256]{5,4,3,2,1,0:T(8,128)(2,1)S(1)} %fusion.9), channel_id=1, source_target_pairs={{0,16},{4,20},{8,24},{12,28},{16,0},{20,4},{24,8},{28,12},{1,17},{... | collective-permute-start | bytes 196616 | tf_op jit(solution)/shard_map/ppermute | solution.py:51
  221.5 4.4 %collective-permute-start.28 = (bf16[1,2,2,16,512]{4,3,2,1,0:T(8,128)(2,1)S(1)}, bf16[1,2,2,16,512]{4,3,2,1,0:T(8,128)(2,1)S(1)}, u32[]{:S(2)}, u32[]{:S(2)}) collective-permute-start(bf16[1,2,2,16,512]{4,3,2,1,0:T(8,128)(2,1)S(1)} %fusion.10), channel_id=1, source_target_pairs={{0,8},{4,12},{8,0},{12,4},{16,24},{20,28},{24,16},{28,20},{1,9},{5... | collective-permute-start | bytes 196616 | tf_op jit(solution)/shard_map/ppermute | solution.py:51
  222.4 4.0 %collective-permute-start.23 = (bf16[1,2,2,16,256]{4,3,2,1,0:T(8,128)(2,1)S(1)}, bf16[1,2,2,16,256]{4,3,2,1,0:T(8,128)(2,1)S(1)}, u32[]{:S(2)}, u32[]{:S(2)}) collective-permute-start(bf16[1,2,2,16,256]{4,3,2,1,0:T(8,128)(2,1)S(1)} %fusion.12), channel_id=1, source_target_pairs={{0,8},{4,12},{8,0},{12,4},{16,24},{20,28},{24,16},{28,20},{1,9},{5... | collective-permute-start | bytes 98312 | tf_op jit(solution)/shard_map/ppermute | solution.py:51
  225.9 5.0 %collective-permute-start.29 = (bf16[1,2,16,512]{3,2,1,0:T(8,128)(2,1)S(1)}, bf16[1,2,16,512]{3,2,1,0:T(8,128)(2,1)S(1)}, u32[]{:S(2)}, u32[]{:S(2)}) collective-permute-start(bf16[1,2,16,512]{3,2,1,0:T(8,128)(2,1)S(1)} %fusion.13), channel_id=1, source_target_pairs={{0,2},{1,3},{2,0},{3,1},{4,6},{5,7},{6,4},{7,5},{8,10},{9,11},{10,... | collective-permute-start | bytes 98312 | tf_op jit(solution)/shard_map/ppermute | solution.py:51
  226.5 4.7 %collective-permute-start.24 = (bf16[1,2,16,256]{3,2,1,0:T(8,128)(2,1)S(1)}, bf16[1,2,16,256]{3,2,1,0:T(8,128)(2,1)S(1)}, u32[]{:S(2)}, u32[]{:S(2)}) collective-permute-start(bf16[1,2,16,256]{3,2,1,0:T(8,128)(2,1)S(1)} %fusion.15), channel_id=1, source_target_pairs={{0,2},{1,3},{2,0},{3,1},{4,6},{5,7},{6,4},{7,5},{8,10},{9,11},{10,... | collective-permute-start | bytes 49160 | tf_op jit(solution)/shard_map/ppermute | solution.py:51
  230.9 3.8 %collective-permute-start.30 = (bf16[1,16,512]{2,1,0:T(8,128)(2,1)S(1)}, bf16[1,16,512]{2,1,0:T(8,128)(2,1)S(1)}, u32[]{:S(2)}, u32[]{:S(2)}) collective-permute-start(bf16[1,16,512]{2,1,0:T(8,128)(2,1)S(1)} %fusion.16), channel_id=1, source_target_pairs={{0,1},{1,0},{2,3},{3,2},{4,5},{5,4},{6,7},{7,6},{8,9},{9,8},{10,11... | collective-permute-start | bytes 49160 | tf_op jit(solution)/shard_map/ppermute | solution.py:51
  231.2 8.6 %collective-permute-start.25 = (bf16[1,16,256]{2,1,0:T(8,128)(2,1)S(1)}, bf16[1,16,256]{2,1,0:T(8,128)(2,1)S(1)}, u32[]{:S(2)}, u32[]{:S(2)}) collective-permute-start(bf16[1,16,256]{2,1,0:T(8,128)(2,1)S(1)} %fusion.22), channel_id=1, source_target_pairs={{0,1},{1,0},{2,3},{3,2},{4,5},{5,4},{6,7},{7,6},{8,9},{9,8},{10,11... | collective-permute-start | bytes 24584 | tf_op jit(solution)/shard_map/ppermute | solution.py:51
  238.0 10.5 %collective-permute-start.37 = (bf16[1,2,2,2,64,512]{5,4,3,2,1,0:T(8,128)(2,1)}, bf16[1,2,2,2,64,512]{5,4,3,2,1,0:T(8,128)(2,1)}, u32[]{:S(2)}, u32[]{:S(2)}) collective-permute-start(bf16[1,2,2,2,64,512]{5,4,3,2,1,0:T(8,128)(2,1)} %fusion.1), channel_id=1, source_target_pairs={{0,8},{4,12},{8,0},{12,4},{16,24},{20,28},{24,16},{28,20},{1,9},{5... | collective-permute-start | bytes 1572872 | tf_op jit(solution)/shard_map/ppermute | solution.py:51
  239.2 15.9 %collective-permute-start.32 = (bf16[5,2,2,2,16,512]{5,4,0,3,2,1:T(8,128)(2,1)S(1)}, bf16[5,2,2,2,16,512]{5,4,0,3,2,1:T(8,128)(2,1)}, u32[]{:S(2)}, u32[]{:S(2)}) collective-permute-start(bf16[5,2,2,2,16,512]{5,4,0,3,2,1:T(8,128)(2,1)S(1)} %fusion), channel_id=1, source_target_pairs={{0,16},{4,20},{8,24},{12,28},{16,0},{20,4},{24,8},{28,12},{1,17},{... | collective-permute-start | bytes 1966088 | tf_op jit(solution)/shard_map/ppermute | solution.py:51
  250.1 7.7 %collective-permute-start.38 = (bf16[1,2,2,64,512]{4,3,2,1,0:T(8,128)(2,1)S(1)}, bf16[1,2,2,64,512]{4,3,2,1,0:T(8,128)(2,1)S(1)}, u32[]{:S(2)}, u32[]{:S(2)}) collective-permute-start(bf16[1,2,2,64,512]{4,3,2,1,0:T(8,128)(2,1)S(1)} %fusion.3), channel_id=1, source_target_pairs={{0,16},{4,20},{8,24},{12,28},{16,0},{20,4},{24,8},{28,12},{1,17},{... | collective-permute-start | bytes 786440 | tf_op jit(solution)/shard_map/ppermute | solution.py:51
  256.5 7.1 %collective-permute-start.33 = (bf16[5,2,2,16,512]{4,3,0,2,1:T(8,128)(2,1)S(1)}, bf16[5,2,2,16,512]{4,3,0,2,1:T(8,128)(2,1)S(1)}, u32[]{:S(2)}, u32[]{:S(2)}) collective-permute-start(bf16[5,2,2,16,512]{4,3,0,2,1:T(8,128)(2,1)S(1)} %fusion.2), channel_id=1, source_target_pairs={{0,8},{4,12},{8,0},{12,4},{16,24},{20,28},{24,16},{28,20},{1,9},{5... | collective-permute-start | bytes 983048 | tf_op jit(solution)/shard_map/ppermute | solution.py:51
  257.9 8.2 %collective-permute-start.39 = (bf16[1,2,64,512]{3,2,1,0:T(8,128)(2,1)S(1)}, bf16[1,2,64,512]{3,2,1,0:T(8,128)(2,1)S(1)}, u32[]{:S(2)}, u32[]{:S(2)}) collective-permute-start(bf16[1,2,64,512]{3,2,1,0:T(8,128)(2,1)S(1)} %fusion.6), channel_id=1, source_target_pairs={{0,2},{1,3},{2,0},{3,1},{4,6},{5,7},{6,4},{7,5},{8,10},{9,11},{10,... | collective-permute-start | bytes 393224 | tf_op jit(solution)/shard_map/ppermute | solution.py:51
  263.8 7.4 %collective-permute-start.34 = (bf16[5,2,16,512]{3,2,0,1:T(8,128)(2,1)S(1)}, bf16[5,2,16,512]{3,2,0,1:T(8,128)(2,1)S(1)}, u32[]{:S(2)}, u32[]{:S(2)}) collective-permute-start(bf16[5,2,16,512]{3,2,0,1:T(8,128)(2,1)S(1)} %fusion.4), channel_id=1, source_target_pairs={{0,2},{1,3},{2,0},{3,1},{4,6},{5,7},{6,4},{7,5},{8,10},{9,11},{10,... | collective-permute-start | bytes 491528 | tf_op jit(solution)/shard_map/ppermute | solution.py:51
  266.1 5.9 %collective-permute-start.40 = (bf16[1,64,512]{2,1,0:T(8,128)(2,1)S(1)}, bf16[1,64,512]{2,1,0:T(8,128)(2,1)S(1)}, u32[]{:S(2)}, u32[]{:S(2)}) collective-permute-start(bf16[1,64,512]{2,1,0:T(8,128)(2,1)S(1)} %fusion.11), channel_id=1, source_target_pairs={{0,1},{1,0},{2,3},{3,2},{4,5},{5,4},{6,7},{7,6},{8,9},{9,8},{10,11... | collective-permute-start | bytes 196616 | tf_op jit(solution)/shard_map/ppermute | solution.py:51
  271.3 4.5 %collective-permute-start.35 = (bf16[5,16,512]{2,1,0:T(8,128)(2,1)S(1)}, bf16[5,16,512]{2,1,0:T(8,128)(2,1)S(1)}, u32[]{:S(2)}, u32[]{:S(2)}) collective-permute-start(bf16[5,16,512]{2,1,0:T(8,128)(2,1)S(1)} %fusion.8), channel_id=1, source_target_pairs={{0,1},{1,0},{2,3},{3,2},{4,5},{5,4},{6,7},{7,6},{8,9},{9,8},{10,11... | collective-permute-start | bytes 245768 | tf_op jit(solution)/shard_map/ppermute | solution.py:51
  (20 other events, 35.6 us)
